TPU v7x, 32 devices: a whole 2x2x4 slice. The times are simulated.
32 devices in a mesh: branch: 4 (over z), row: 4 (over y, x), col: 2 (over core).
Axes of the slice: x: 2, y: 2, z: 4, core: 2. Of those that a mesh axis runs over, the one named last changes fastest.
Arguments:
- alignment: bfloat16 [64, 128, 256], P(('branch', 'row'), 'col'), may hold values from -32 to 32
- pair_features: bfloat16 [128, 128, 128], P('col', 'row'), may hold values from -32 to 32
- w_row: bfloat16 [256, 1024], replicated, may hold values from -8 to 8
- row_output_weight: bfloat16 [256, 256], replicated, may hold values from -1.5 to 1.5
- w_bias: bfloat16 [128, 8], replicated, may hold values from -1 to 1
- w_column: bfloat16 [256, 1024], replicated, may hold values from -8 to 8
- column_output_weight: bfloat16 [256, 256], replicated, may hold values from -1.5 to 1.5
- outer_input_weight: bfloat16 [256, 64], replicated, may hold values from -0.375 to 0.375
- w_outer_out: bfloat16 [1024, 128], replicated, may hold values from -1.5 to 1.5
- w_triangle_in: bfloat16 [128, 512], replicated, may hold values from -0.5 to 0.5
- w_triangle_gate: bfloat16 [128, 128], replicated, may hold values from -0.5 to 0.5
- w_triangle_out: bfloat16 [128, 128], replicated, may hold values from -0.5 to 0.5
Outputs:
- alignment_out: bfloat16 [64, 128, 256], P(('branch', 'row'), 'col')
- pair_out: bfloat16 [128, 128, 128], P('col', 'row', 'branch')
All inputs are finite; a program needn't handle non-finite values.
Results may differ from a plain program's by a relative error of at most 0.013.
Values may be sent and summed in bfloat16 or wider, within the bound.
A program may use at most 64 MiB of HBM per device.

v0:
```python
import jax
import jax.numpy as jnp
from jax import lax
from jax.sharding import PartitionSpec as P

ALIGN_CHANNELS = 256
PAIR_WIDTH = 128
HEAD_COUNT = 8
HEAD_CHANNELS = 32
FACTOR_CHANNELS = 32
TRIANGLE_WIDTH = 128


EPSILON = 1e-05


def layer_norm(inputs):
    inputs = inputs.astype(jnp.float32)
    average = jnp.mean(inputs, axis=-1, keepdims=True)
    variance = jnp.mean(jnp.square(inputs - average), axis=-1, keepdims=True)
    return (inputs - average) * lax.rsqrt(variance + EPSILON)


def project(normed_input, weight_matrix):
    flat_rows = normed_input.reshape(-1, normed_input.shape[-1])
    result = jnp.dot(flat_rows, weight_matrix, preferred_element_type=jnp.float32)
    return result.reshape(normed_input.shape[:-1] + (weight_matrix.shape[1],))


def split_heads(row_entries):
    return row_entries.reshape(row_entries.shape[:-1] + (HEAD_COUNT, HEAD_CHANNELS))


def attend(query_matrix, key_matrix, value_matrix, head_bias, seq_major):
    query_heads = split_heads(query_matrix)
    key_heads = split_heads(key_matrix)
    value_heads = split_heads(value_matrix)
    if seq_major:
        scores = jnp.einsum(
            "qbhd,kbhd->bhqk", query_heads, key_heads, preferred_element_type=jnp.float32
        )
    else:
        scores = jnp.einsum(
            "bqhd,bkhd->bhqk", query_heads, key_heads, preferred_element_type=jnp.float32
        )
    if head_bias is not None:
        scores = scores + head_bias.astype(jnp.float32)[None]
    attention = jax.nn.softmax(scores, axis=-1).astype(jnp.bfloat16)
    if seq_major:
        mixed_channels = jnp.einsum(
            "bhqk,kbhd->qbhd", attention, value_heads, preferred_element_type=jnp.float32
        )
    else:
        mixed_channels = jnp.einsum(
            "bhqk,bkhd->bqhd", attention, value_heads, preferred_element_type=jnp.float32
        )
    return mixed_channels.reshape(mixed_channels.shape[:2] + (ALIGN_CHANNELS,))


def column_attention(row_entries, weight_matrix, output_weight):
    normed_input = layer_norm(row_entries).astype(jnp.bfloat16)
    projected_input = project(normed_input, weight_matrix)
    query_matrix = (projected_input[..., :ALIGN_CHANNELS] * HEAD_CHANNELS ** (-0.5)).astype(
        jnp.bfloat16
    )
    key_matrix = projected_input[..., ALIGN_CHANNELS : 2 * ALIGN_CHANNELS].astype(jnp.bfloat16)
    value_matrix = projected_input[..., 2 * ALIGN_CHANNELS : 3 * ALIGN_CHANNELS].astype(
        jnp.bfloat16
    )
    gate_values = jax.nn.sigmoid(projected_input[..., 3 * ALIGN_CHANNELS :])
    attended = attend(query_matrix, key_matrix, value_matrix, None, True)
    gated_output = (gate_values * attended).astype(jnp.bfloat16)
    return (row_entries.astype(jnp.float32) + project(gated_output, output_weight)).astype(
        jnp.bfloat16
    )


def outer_mean(left_factor, right_factor, w_outer_out):
    seq_count = left_factor.shape[0]
    outer_sum = jnp.einsum(
        "sic,sje->ijce", left_factor, right_factor, preferred_element_type=jnp.float32
    ) * (1.0 / seq_count)
    flat_rows = outer_sum.reshape(-1, FACTOR_CHANNELS * FACTOR_CHANNELS).astype(jnp.bfloat16)
    residual_update = jnp.dot(flat_rows, w_outer_out, preferred_element_type=jnp.float32)
    return residual_update.reshape(outer_sum.shape[:2] + (PAIR_WIDTH,)).astype(jnp.bfloat16)


def local(
    alignment,
    pair_features,
    w_row,
    row_output_weight,
    w_bias,
    w_column,
    column_output_weight,
    outer_input_weight,
    w_outer_out,
    w_triangle_in,
    w_triangle_gate,
    w_triangle_out,
):
    pair_normed = layer_norm(pair_features).astype(jnp.bfloat16)
    bias_tile = jnp.einsum(
        "ijc,ch->hij", pair_normed, w_bias, preferred_element_type=jnp.float32
    ).astype(jnp.bfloat16)
    head_bias = lax.all_gather(bias_tile, "row", axis=2, tiled=True)
    row_normed = layer_norm(alignment).astype(jnp.bfloat16)
    local_weight = jnp.concatenate(
        [w_row[:, :ALIGN_CHANNELS], w_row[:, 3 * ALIGN_CHANNELS :]], axis=1
    )
    local_projected = project(row_normed, local_weight)
    query_matrix = (local_projected[..., :ALIGN_CHANNELS] * HEAD_CHANNELS ** (-0.5)).astype(
        jnp.bfloat16
    )
    gate_values = jax.nn.sigmoid(local_projected[..., ALIGN_CHANNELS:])
    gathered = lax.all_gather(row_normed, "col", axis=1, tiled=True)
    key_value = project(gathered, w_row[:, ALIGN_CHANNELS : 3 * ALIGN_CHANNELS]).astype(
        jnp.bfloat16
    )
    key_matrix = key_value[..., :ALIGN_CHANNELS]
    value_matrix = key_value[..., ALIGN_CHANNELS:]
    attended = attend(query_matrix, key_matrix, value_matrix, head_bias, False)
    row_gated = (gate_values * attended).astype(jnp.bfloat16)
    alignment_row = (alignment.astype(jnp.float32) + project(row_gated, row_output_weight)).astype(
        jnp.bfloat16
    )
    columns = lax.all_to_all(
        alignment_row, ("branch", "row"), split_axis=1, concat_axis=0, tiled=True
    )
    column_new = column_attention(columns, w_column, column_output_weight)
    alignment_out = lax.all_to_all(
        column_new, ("branch", "row"), split_axis=0, concat_axis=1, tiled=True
    )
    outer_normed_input = layer_norm(alignment_out).astype(jnp.bfloat16)
    factor_pairs = project(outer_normed_input, outer_input_weight).astype(jnp.bfloat16)
    left_factor = lax.all_gather(
        factor_pairs[..., :FACTOR_CHANNELS], ("branch", "row"), axis=0, tiled=True
    )
    right_columns = lax.all_gather(factor_pairs[..., FACTOR_CHANNELS:], "col", axis=1, tiled=True)
    right_rows = lax.all_to_all(right_columns, "row", split_axis=1, concat_axis=0, tiled=True)
    right_factor = lax.all_gather(right_rows, "branch", axis=0, tiled=True)
    outer_update = outer_mean(left_factor, right_factor, w_outer_out)
    pair_mid = (pair_features.astype(jnp.float32) + outer_update.astype(jnp.float32)).astype(
        jnp.bfloat16
    )
    tile_first, tile_second, _ = pair_mid.shape
    groups = lax.axis_size("branch")
    branch_width = TRIANGLE_WIDTH // groups
    branch_start = lax.axis_index("branch") * branch_width
    out_width = PAIR_WIDTH // groups
    out_start = lax.axis_index("branch") * out_width
    triangle_normed = layer_norm(pair_mid).astype(jnp.bfloat16)
    flat_normed = triangle_normed.reshape(-1, PAIR_WIDTH)
    w_in = lax.dynamic_slice_in_dim(
        w_triangle_in.reshape(PAIR_WIDTH, 4, TRIANGLE_WIDTH), branch_start, branch_width, 2
    )
    w_in = w_in.reshape(PAIR_WIDTH, 4 * branch_width)
    tri_projected = jnp.dot(flat_normed, w_in, preferred_element_type=jnp.float32)
    tri_projected = tri_projected.reshape(tile_first, tile_second, 4, branch_width)
    tri_left = (jax.nn.sigmoid(tri_projected[:, :, 1]) * tri_projected[:, :, 0]).astype(
        jnp.bfloat16
    )
    tri_right = (jax.nn.sigmoid(tri_projected[:, :, 3]) * tri_projected[:, :, 2]).astype(
        jnp.bfloat16
    )
    left_channels = jnp.transpose(tri_left, (2, 0, 1))
    right_channels = jnp.transpose(tri_right, (2, 0, 1))
    right_full = lax.all_gather(right_channels, "col", axis=1, tiled=True)
    right_keys = lax.all_to_all(right_full, "row", split_axis=1, concat_axis=2, tiled=True)
    product = jnp.einsum(
        "cik,cjk->cij",
        lax.all_gather(left_channels, "row", axis=2, tiled=True),
        right_keys,
        preferred_element_type=jnp.float32,
    )
    triangle_sum = jnp.transpose(product, (1, 2, 0)).astype(jnp.bfloat16)
    gate_weight = lax.dynamic_slice_in_dim(w_triangle_gate, out_start, out_width, 1)
    output_gate = jax.nn.sigmoid(
        jnp.dot(flat_normed, gate_weight, preferred_element_type=jnp.float32)
    )
    all_channels = lax.all_gather(triangle_sum, "branch", axis=2, tiled=True)
    triangle_scaled = layer_norm(all_channels).astype(jnp.bfloat16)
    column_weight = lax.dynamic_slice_in_dim(w_triangle_out, out_start, out_width, 1)
    mixed_channels = jnp.dot(
        triangle_scaled.reshape(-1, TRIANGLE_WIDTH),
        column_weight,
        preferred_element_type=jnp.float32,
    )
    pair_slice = lax.dynamic_slice_in_dim(pair_mid, out_start, out_width, 2).reshape(-1, out_width)
    pair_out = (pair_slice.astype(jnp.float32) + output_gate * mixed_channels).astype(jnp.bfloat16)
    return (alignment_out, pair_out.reshape(tile_first, tile_second, out_width))


def solution(mesh):
    in_specs = (
        P(("branch", "row"), "col", None),
        P("col", "row", None),
        P(),
        P(),
        P(),
        P(),
        P(),
        P(),
        P(),
        P(),
        P(),
        P(),
    )
    out_specs = (P(("branch", "row"), "col", None), P("col", "row", "branch"))
    return jax.shard_map(local, mesh=mesh, in_specs=in_specs, out_specs=out_specs, check_vma=False)
```

profile of v0, /device:TPU:0, one launch (start us, length us, event | category | flops | bytes accessed | tf_op | source)
XLA Modules:
  0.0 211.0 jit_solution(17436135564656589081)
XLA Ops:
  0.7 1.8 copy.146
  3.8 10.4 %all_gather.25 = bf16[8,64,128]{1,0,2:T(8,128)(2,1)S(1)} all-gather(bf16[8,64,32]{1,0,2:T(8,128)(2,1)S(1)} %copy.148), channel_id=1, replica_groups=mesh['branch'=4,'row'=4,'col'=2] {'row'}, dimensions={2}, use_global_device_ids=true | all-gather | bytes 163840 | tf_op jit(solution)/shard_map/all_gather | solution.py:106
  15.0 2.0 all_gather.24
  20.0 1.4 convolution_add_fusion
  21.4 1.8 fusion.103
  23.2 1.1 copy.143
  24.3 4.4 %fusion.44 = f32[4,8,32,64]{3,2,1,0:T(8,128)} fusion(bf16[4,128,8,32]{1,3,2,0:T(8,128)(2,1)S(1)} %bitcast.162, f32[4,8,64]{2,1,0:T(8,128)S(1)} %fusion.103, f32[4,8,64,128]{3,2,1,0:T(8,128)S(1)} %convolution_add_fusion), kind=kOutput, calls=%fused_computation.67 | convolution fusion | flops 17565824 | bytes 1581056 | tf_op jit(solution)/shard_map/bhqk,bkhd->bqhd/dot_general | solution.py:54
  28.8 1.2 copy.150
  30.0 1.1 fusion.23
  31.2 13.5 %all_to_all.63 = bf16[4,64,256]{2,0,1:T(4,128)(2,1)S(1)} all-to-all(bf16[4,64,256]{2,0,1:T(4,128)(2,1)S(1)} %copy.151), channel_id=1, replica_groups=mesh['branch'=4,'row'=4,'col'=2] {'branch','row'}, dimensions={1} | all-to-all | bytes 262144 | tf_op jit(solution)/shard_map/all_to_all | solution.py:127
  47.4 1.3 fusion.106
  50.1 2.0 fusion.45
  52.9 1.2 fusion.24
  54.9 3.5 %all-to-all-start.1 = ((bf16[64,4,256]{2,1,0:T(4,128)(2,1)}), bf16[64,4,256]{2,1,0:T(4,128)(2,1)S(1)}, u32[]{:S(2)}, u32[]{:S(2)}) async-start(bf16[64,4,256]{2,1,0:T(4,128)(2,1)} %copy.164), calls=%async_computation.1 | async-start | bytes 262144 | tf_op jit(solution)/shard_map/all_to_all | solution.py:131
  58.7 7.5 %all-to-all-done.1 = bf16[64,4,256]{2,1,0:T(4,128)(2,1)S(1)} async-done(((bf16[64,4,256]{2,1,0:T(4,128)(2,1)}), bf16[64,4,256]{2,1,0:T(4,128)(2,1)S(1)}, u32[]{:S(2)}, u32[]{:S(2)}) %all-to-all-start.1) | async-done | bytes 131104 | tf_op jit(solution)/shard_map/all_to_all | solution.py:131
  67.8 1.9 all_gather.26
  70.5 3.3 %all-to-all-start.2 = ((bf16[4,2,2048]{2,1,0:T(2,128)(2,1)}), bf16[4,2,2048]{2,1,0:T(2,128)(2,1)S(1)}, u32[]{:S(2)}, u32[]{:S(2)}) async-start(bf16[4,2,2048]{2,1,0:T(2,128)(2,1)} %reshape.271), calls=%async_computation.2 | async-start | bytes 65536 | tf_op jit(solution)/shard_map/all_to_all | solution.py:140
  73.7 42.2 %all_gather.28 = bf16[64,64,32]{1,2,0:T(8,128)(2,1)S(1)} all-gather(bf16[4,64,32]{1,2,0:T(8,128)(2,1)S(1)} %get-tuple-element.22), channel_id=1, replica_groups=mesh['branch'=4,'row'=4,'col'=2] {'branch','row'}, dimensions={0}, use_global_device_ids=true | all-gather | bytes 278528 | tf_op jit(solution)/shard_map/all_gather | solution.py:136
  116.1 15.0 %all_gather.27 = bf16[64,32,32]{2,0,1:T(8,128)(2,1)S(1)} all-gather(bf16[16,32,32]{2,0,1:T(8,128)(2,1)S(1)} %bitcast.156), channel_id=1, replica_groups=mesh['branch'=4,'row'=4,'col'=2] {'branch'}, dimensions={0}, use_global_device_ids=true | all-gather | bytes 163840 | tf_op jit(solution)/shard_map/all_gather | solution.py:141
  131.1 2.7 %multiply_convert_fusion = bf16[32,32,64,32]{2,1,3,0:T(8,128)(2,1)S(1)} fusion(bf16[64,32,32]{2,0,1:T(8,128)(2,1)S(1)} %all_gather.27, bf16[64,64,32]{1,2,0:T(8,128)(2,1)S(1)} %all_gather.28), kind=kOutput, calls=%fused_computation.2 | convolution fusion | flops 272629760 | bytes 4587520 | tf_op jit(solution)/shard_map/sic,sje->ijce/dot_general | solution.py:80
  133.8 1.4 convert_reduce_fusion.1
  136.1 1.4 fusion.14
  140.7 2.6 %all_gather.30 = bf16[32,128,32]{2,0,1:T(8,128)(2,1)S(1)} all-gather(bf16[32,64,32]{2,0,1:T(8,128)(2,1)S(1)} %copy.181), channel_id=1, replica_groups=mesh['branch'=4,'row'=4,'col'=2] {'col'}, dimensions={1}, use_global_device_ids=true | all-gather | bytes 393216 | tf_op jit(solution)/shard_map/all_gather | solution.py:168
  143.3 1.7 reshape.273
  144.9 3.4 %all-to-all-start.3 = ((bf16[4,2,16384]{2,1,0:T(2,128)(2,1)}), bf16[4,2,16384]{2,1,0:T(2,128)(2,1)S(1)}, u32[]{:S(2)}, u32[]{:S(2)}) async-start(bf16[4,2,16384]{2,1,0:T(2,128)(2,1)} %reshape.273), calls=%async_computation.3 | async-start | bytes 524288 | tf_op jit(solution)/shard_map/all_to_all | solution.py:169
  148.3 24.7 %all_gather.29 = bf16[32,64,128]{0,2,1:T(8,128)(2,1)S(1)} all-gather(bf16[32,64,32]{0,2,1:T(8,128)(2,1)S(1)} %get-tuple-element.12), channel_id=1, replica_groups=mesh['branch'=4,'row'=4,'col'=2] {'row'}, dimensions={2}, use_global_device_ids=true | all-gather | bytes 655360 | tf_op jit(solution)/shard_map/all_gather | solution.py:172
  173.0 3.9 %copy.183 = bf16[32,64,128]{1,2,0:T(8,128)(2,1)} copy(bf16[32,64,128]{0,2,1:T(8,128)(2,1)S(1)} %all_gather.29) | data formatting | bytes 1048576 | tf_op jit(solution)/shard_map/all_gather | solution.py:172
  176.9 2.0 copy.178
  180.7 1.8 copy.220
  182.6 2.0 all_to_all.58
  184.9 20.8 %all_gather.31 = bf16[64,32,128]{0,1,2:T(8,128)(2,1)S(1)} all-gather(bf16[64,32,32]{0,1,2:T(8,128)(2,1)S(1)} %fusion.22), channel_id=1, replica_groups=mesh['branch'=4,'row'=4,'col'=2] {'branch'}, dimensions={2}, use_global_device_ids=true | all-gather | bytes 655360 | tf_op jit(solution)/shard_map/all_gather | solution.py:181
  205.7 1.5 copy.184
  (115 shorter events, 23.3 us)
Async XLA Ops:
  0.6 45.3 %copy-start = (bf16[256,1024]{1,0:T(8,128)(2,1)S(1)}, bf16[256,1024]{1,0:T(8,128)(2,1)}, u32[]{:S(2)}) copy-start(bf16[256,1024]{1,0:T(8,128)(2,1)} %param.17) | copy-start | bytes 1572868
  0.6 2.5 %copy-start.12 = (bf16[128,8]{0,1:T(8,128)(2,1)S(1)}, bf16[128,8]{0,1:T(8,128)(2,1)}, u32[]{:S(2)}) copy-start(bf16[128,8]{0,1:T(8,128)(2,1)} %param.16) | copy-start | bytes 6148
  2.7 11.8 %copy-start.3 = (bf16[4,64,256]{2,1,0:T(8,128)(2,1)S(1)}, bf16[4,64,256]{2,1,0:T(8,128)(2,1)}, u32[]{:S(2)}) copy-start(bf16[4,64,256]{2,1,0:T(8,128)(2,1)} %param.12) | copy-start | bytes 393220
  3.1 11.9 %copy-start.5 = (bf16[256,1024]{1,0:T(8,128)(2,1)S(1)}, bf16[256,1024]{1,0:T(8,128)(2,1)}, u32[]{:S(2)}) copy-start(bf16[256,1024]{1,0:T(8,128)(2,1)} %param.14) | copy-start | bytes 1572868
  47.4 1.8 copy-start.4
  52.0 6.4 %copy-start.6 = (bf16[128,512]{1,0:T(8,128)(2,1)S(1)}, bf16[128,512]{1,0:T(8,128)(2,1)}, u32[]{:S(2)}) copy-start(bf16[128,512]{1,0:T(8,128)(2,1)} %param.21) | copy-start | bytes 393220
  52.9 14.4 %copy-start.10 = (bf16[256,64]{0,1:T(8,128)(2,1)S(1)}, bf16[256,64]{0,1:T(8,128)(2,1)}, u32[]{:S(2)}) copy-start(bf16[256,64]{0,1:T(8,128)(2,1)} %param.19) | copy-start | bytes 98308
  54.9 11.3 %all-to-all-start.1 = ((bf16[64,4,256]{2,1,0:T(4,128)(2,1)}), bf16[64,4,256]{2,1,0:T(4,128)(2,1)S(1)}, u32[]{:S(2)}, u32[]{:S(2)}) async-start(bf16[64,4,256]{2,1,0:T(4,128)(2,1)} %copy.164), calls=%async_computation.1 | async-start | bytes 262144 | tf_op jit(solution)/shard_map/all_to_all | solution.py:131
  67.3 66.5 %copy-start.7 = (bf16[4,64,256]{2,1,0:T(8,128)(2,1)}, bf16[4,64,256]{2,1,0:T(8,128)(2,1)S(1)}, u32[]{:S(2)}) copy-start(bf16[4,64,256]{2,1,0:T(8,128)(2,1)S(1)} %all_to_all.50) | copy-start | bytes 393220
  70.5 45.5 %all-to-all-start.2 = ((bf16[4,2,2048]{2,1,0:T(2,128)(2,1)}), bf16[4,2,2048]{2,1,0:T(2,128)(2,1)S(1)}, u32[]{:S(2)}, u32[]{:S(2)}) async-start(bf16[4,2,2048]{2,1,0:T(2,128)(2,1)} %reshape.271), calls=%async_computation.2 | async-start | bytes 65536 | tf_op jit(solution)/shard_map/all_to_all | solution.py:140
  131.1 2.7 %copy-start.9 = (bf16[1024,128]{1,0:T(8,128)(2,1)S(1)}, bf16[1024,128]{1,0:T(8,128)(2,1)}, u32[]{:S(2)}) copy-start(bf16[1024,128]{1,0:T(8,128)(2,1)} %param.20) | copy-start | bytes 786436
  144.9 35.3 %all-to-all-start.3 = ((bf16[4,2,16384]{2,1,0:T(2,128)(2,1)}), bf16[4,2,16384]{2,1,0:T(2,128)(2,1)S(1)}, u32[]{:S(2)}, u32[]{:S(2)}) async-start(bf16[4,2,16384]{2,1,0:T(2,128)(2,1)} %reshape.273), calls=%async_computation.3 | async-start | bytes 524288 | tf_op jit(solution)/shard_map/all_to_all | solution.py:169
  173.0 5.9 %copy-start.2 = (f32[64,32,32]{0,2,1:T(8,128)S(1)}, f32[64,32,32]{0,2,1:T(8,128)}, u32[]{:S(2)}) copy-start(f32[64,32,32]{0,2,1:T(8,128)} %dynamic-slice_convert_fusion) | copy-start | bytes 786436
  176.9 2.9 %copy-start.11 = (bf16[128,128]{1,0:T(8,128)(2,1)S(1)}, bf16[128,128]{1,0:T(8,128)(2,1)}, u32[]{:S(2)}) copy-start(bf16[128,128]{1,0:T(8,128)(2,1)} %param.22) | copy-start | bytes 98308
  180.2 4.3 %copy-start.1 = (bf16[32,64,128]{1,2,0:T(8,128)(2,1)S(1)}, bf16[32,64,128]{1,2,0:T(8,128)(2,1)}, u32[]{:S(2)}) copy-start(bf16[32,64,128]{1,2,0:T(8,128)(2,1)} %copy.183) | copy-start | bytes 1572868
  205.7 3.5 %copy-start.8 = (bf16[128,128]{1,0:T(8,128)(2,1)S(1)}, bf16[128,128]{1,0:T(8,128)(2,1)}, u32[]{:S(2)}) copy-start(bf16[128,128]{1,0:T(8,128)(2,1)} %param.23) | copy-start | bytes 98308
where the time goes:
time: 212 us; the launch traced here: 211 us
  blocking collectives  133 us (63%)
  local copies, waits for them, and re-layouts  30.6 us (14%)
  matrix products  21.2 us (10%)
  starting transfers between devices  10.2 us (5%)
  waiting for transfers between devices  7.47 us (4%)
  other arithmetic  7.29 us (3%)
    all_gather x1, blocking collectives, local(): lax.all_gather(factor_pairs[..., :FACTOR_CHANNELS], ('branch', 'row'), ax...  42.2 us
    all_gather x1, blocking collectives, local(): lax.all_gather(left_channels, 'row', axis=2, tiled=True)  24.7 us
    all_gather x1, blocking collectives, local(): all_channels = lax.all_gather(triangle_sum, 'branch', axis=2, tiled=True)  20.8 us
    all_gather x1, blocking collectives, local(): right_factor = lax.all_gather(right_rows, 'branch', axis=0, tiled=True)  15 us
    all_to_all x1, blocking collectives, local(): lax.all_to_all(alignment_row, ('branch', 'row'), split_axis=1, concat_axi...  13.5 us
    all_gather x1, blocking collectives, local(): head_bias = lax.all_gather(bias_tile, 'row', axis=2, tiled=True)  10.4 us
    all_to_all x1, waiting for transfers between devices, local(): lax.all_to_all(column_new, ('branch', 'row'), split_axis=0, concat_axis=1...  7.46 us
    unnamed x34, local copies, waits for them, and re-layouts  6.15 us
  transfers between devices with their start and end apart: 3, of which 1 were waited for; matrix products, arithmetic and copies ran while one was open for 4% of the time, Pallas kernels for 0%

commit v1 on v0

--- a/solution.py
+++ b/solution.py
@@ -1,6 +1,10 @@
+import functools
+
 import jax
 import jax.numpy as jnp
 from jax import lax
+from jax.experimental import pallas as pl
+from jax.experimental.pallas import tpu as pltpu
 from jax.sharding import PartitionSpec as P
 
 ALIGN_CHANNELS = 256
@@ -83,6 +87,332 @@
     flat_rows = outer_sum.reshape(-1, FACTOR_CHANNELS * FACTOR_CHANNELS).astype(jnp.bfloat16)
     residual_update = jnp.dot(flat_rows, w_outer_out, preferred_element_type=jnp.float32)
     return residual_update.reshape(outer_sum.shape[:2] + (PAIR_WIDTH,)).astype(jnp.bfloat16)
+
+MESH = pl.DeviceIdType.MESH
+
+
+def group_size(axes):
+    size = 1
+    for axis in axes:
+        size *= lax.axis_size(axis)
+    return size
+
+
+def group_index(axes):
+    index = 0
+    for axis in axes:
+        index = index * lax.axis_size(axis) + lax.axis_index(axis)
+    return index
+
+
+def group_device(axes, index):
+    device = {}
+    for axis in reversed(axes):
+        size = lax.axis_size(axis)
+        device[axis] = lax.rem(index, size)
+        index = index // size
+    return device
+
+
+def each_peer(axes, action):
+    size = group_size(axes)
+    me = group_index(axes)
+
+    def step(offset, carry):
+        action(offset, lax.rem(me + offset, size), lax.rem(me + size - offset, size))
+        return carry
+
+    if size <= 16:
+        for offset in range(1, size):
+            step(offset, 0)
+    else:
+        lax.fori_loop(1, size, step, 0)
+
+
+def greet(axes):
+    barrier = pltpu.get_barrier_semaphore()
+    each_peer(
+        axes,
+        lambda offset, to, source: pl.semaphore_signal(
+            barrier, inc=1, device_id=group_device(axes, to), device_id_type=MESH
+        ),
+    )
+    return group_size(axes) - 1
+
+
+class Regular:
+    def __init__(self, axes, scatter):
+        self.axes, self.scatter = axes, scatter
+
+    def semaphores(self):
+        size = group_size(self.axes)
+        return [pltpu.SemaphoreType.DMA((size,)), pltpu.SemaphoreType.DMA((size,))]
+
+    def slots(self, x):
+        return x if self.scatter else jax.ShapeDtypeStruct(
+            (group_size(self.axes),) + x.shape, x.dtype
+        )
+
+    def greet(self):
+        return greet(self.axes)
+
+    def block(self, ref, index):
+        return ref.at[index] if self.scatter else ref
+
+    def copy(self, src, dst, sems, offset, to):
+        return pltpu.make_async_remote_copy(
+            src_ref=self.block(src, to),
+            dst_ref=dst.at[group_index(self.axes)],
+            send_sem=sems[0].at[offset],
+            recv_sem=sems[1].at[offset],
+            device_id=group_device(self.axes, to),
+            device_id_type=MESH,
+        )
+
+    def own(self, src, dst, sems):
+        me = group_index(self.axes)
+        return pltpu.make_async_copy(self.block(src, me), dst.at[me], sems[1].at[0])
+
+    def start(self, src, dst, sems):
+        each_peer(
+            self.axes,
+            lambda offset, to, source: self.copy(src, dst, sems, offset, to).start(),
+        )
+        self.own(src, dst, sems).start()
+
+    def wait(self, src, dst, sems):
+        self.own(src, dst, sems).wait()
+
+        def finish(offset, to, source):
+            arriving = pltpu.make_async_remote_copy(
+                src_ref=self.block(src, to),
+                dst_ref=dst.at[source],
+                send_sem=sems[0].at[offset],
+                recv_sem=sems[1].at[offset],
+                device_id=group_device(self.axes, to),
+                device_id_type=MESH,
+            )
+            arriving.wait_send()
+            arriving.wait_recv()
+
+        each_peer(self.axes, finish)
+
+
+class ColToRow:
+    def __init__(self, split):
+        self.split = split
+
+    def sizes(self):
+        rows, cols = lax.axis_size("row"), lax.axis_size("col")
+        return rows, cols, rows // cols
+
+    def sends(self):
+        rows, cols, per = self.sizes()
+        return lax.axis_size("branch") * cols if self.split else per * cols
+
+    def receives(self):
+        rows, cols, per = self.sizes()
+        return lax.axis_size("branch") * rows // per if self.split else rows
+
+    def semaphores(self):
+        return [
+            pltpu.SemaphoreType.DMA((self.sends(),)),
+            pltpu.SemaphoreType.DMA((self.receives(),)),
+            pltpu.SemaphoreType.DMA((1,)),
+        ]
+
+    def slots(self, x):
+        shape = x.shape if self.split else x.shape[1:]
+        return jax.ShapeDtypeStruct((self.receives(),) + shape, x.dtype)
+
+    def target(self, k):
+        rows, cols, per = self.sizes()
+        branch, row, col = (lax.axis_index(a) for a in ("branch", "row", "col"))
+        if self.split:
+            group = branch * rows + row
+            part = lax.axis_size("branch") * rows // per
+            return k // cols, col * per + group // part, k % cols
+        return branch, col * per + k // cols, k % cols
+
+    def slot(self):
+        rows, cols, per = self.sizes()
+        if self.split:
+            group = lax.axis_index("branch") * rows + lax.axis_index("row")
+            return lax.rem(group, lax.axis_size("branch") * rows // per)
+        return lax.axis_index("row")
+
+    def origin(self, k):
+        rows, cols, per = self.sizes()
+        row = lax.axis_index("row")
+        if self.split:
+            part = lax.axis_size("branch") * rows // per
+            group = lax.rem(row, per) * part + k
+            return group // rows, lax.rem(group, rows), row // per
+        return lax.axis_index("branch"), k, row // per
+
+    def mine(self, device):
+        same = device[0] == lax.axis_index("branch")
+        same = jnp.logical_and(same, device[1] == lax.axis_index("row"))
+        return jnp.logical_and(same, device[2] == lax.axis_index("col"))
+
+    def loop(self, count, body):
+        if count <= 16:
+            for k in range(count):
+                body(k)
+        else:
+            lax.fori_loop(0, count, lambda k, carry: (body(k), carry)[1], 0)
+
+    def each(self, count, device_of, away, here=None):
+        def body(k):
+            device = device_of(k)
+            mine = self.mine(device)
+            pl.when(jnp.logical_not(mine))(lambda: away(k, device))
+            if here is not None:
+                pl.when(mine)(lambda: here(k))
+
+        self.loop(count, body)
+
+    def greet(self):
+        barrier = pltpu.get_barrier_semaphore()
+
+        def signal(k, device):
+            pl.semaphore_signal(barrier, inc=1, device_id=device, device_id_type=MESH)
+
+        self.each(self.sends(), self.target, signal)
+        self.each(self.receives(), self.origin, signal)
+        rows, cols, per = self.sizes()
+        row = lax.axis_index("row")
+        if self.split:
+            part = lax.axis_size("branch") * rows // per
+            aimed = lax.axis_index("col") * per + group_index(("branch", "row")) // part
+            mine = (aimed == row).astype(jnp.int32)
+        else:
+            mine = (row // per == lax.axis_index("col")).astype(jnp.int32)
+        return self.sends() + self.receives() - 2 * mine
+
+    def block(self, src, k):
+        if self.split:
+            return src
+        return src.at[k // self.sizes()[1]]
+
+    def start(self, src, dst, sems):
+        def away(k, device):
+            pltpu.make_async_remote_copy(
+                src_ref=self.block(src, k),
+                dst_ref=dst.at[self.slot()],
+                send_sem=sems[0].at[k],
+                recv_sem=sems[1].at[self.slot()],
+                device_id=device,
+                device_id_type=MESH,
+            ).start()
+
+        def here(k):
+            pltpu.make_async_copy(self.block(src, k), dst.at[self.slot()], sems[2].at[0]).start()
+
+        self.each(self.sends(), self.target, away, here)
+
+    def wait(self, src, dst, sems):
+        def sent(k, device):
+            pltpu.make_async_remote_copy(
+                src_ref=self.block(src, k),
+                dst_ref=dst.at[self.slot()],
+                send_sem=sems[0].at[k],
+                recv_sem=sems[1].at[self.slot()],
+                device_id=device,
+                device_id_type=MESH,
+            ).wait_send()
+
+        def here(k):
+            pltpu.make_async_copy(self.block(src, k), dst.at[self.slot()], sems[2].at[0]).wait()
+
+        def arrived(k, device):
+            pltpu.make_async_remote_copy(
+                src_ref=self.block(src, 0),
+                dst_ref=dst.at[k],
+                send_sem=sems[0].at[0],
+                recv_sem=sems[1].at[k],
+                device_id=device,
+                device_id_type=MESH,
+            ).wait_recv()
+
+        self.each(self.sends(), self.target, sent, here)
+        self.each(self.receives(), self.origin, arrived)
+
+
+def exchange_kernel(moves, *refs):
+    count = len(moves)
+    sources, slots, rest = refs[:count], refs[count : 2 * count], list(refs[2 * count :])
+    sems = []
+    for move in moves:
+        width = len(move.semaphores())
+        sems.append(rest[:width])
+        rest = rest[width:]
+    total = 0
+    for move in moves:
+        total += move.greet()
+    pl.semaphore_wait(pltpu.get_barrier_semaphore(), total)
+    for move, source, slot, sem in zip(moves, sources, slots, sems):
+        move.start(source, slot, sem)
+    for move, source, slot, sem in zip(moves, sources, slots, sems):
+        move.wait(source, slot, sem)
+
+
+def exchange(collective_id, moves, arrays):
+    scratch = []
+    for move in moves:
+        scratch += move.semaphores()
+    slots = [move.slots(x) for move, x in zip(moves, arrays)]
+    any_space = pl.BlockSpec(memory_space=pl.ANY)
+    return pl.pallas_call(
+        functools.partial(exchange_kernel, moves),
+        out_shape=[jax.ShapeDtypeStruct(s.shape, s.dtype) for s in slots],
+        in_specs=[any_space] * len(moves),
+        out_specs=[any_space] * len(moves),
+        scratch_shapes=scratch,
+        compiler_params=pltpu.CompilerParams(
+            collective_id=collective_id, has_side_effects=True
+        ),
+    )(*arrays)
+
+
+def mix_kernel(sums_ref, weight_ref, out_ref, held, mixed, *sems):
+    move = Regular(("branch",), True)
+    pl.semaphore_wait(pltpu.get_barrier_semaphore(), move.greet())
+    move.start(sums_ref, held, sems[:2])
+    move.wait(sums_ref, held, sems[:2])
+    sums = held[...].astype(jnp.float32).reshape(-1, held.shape[-1])
+    average = jnp.mean(sums, axis=0, keepdims=True)
+    centred = sums - average
+    variance = jnp.mean(jnp.square(centred), axis=0, keepdims=True)
+    scaled = (centred * lax.rsqrt(variance + EPSILON)).astype(jnp.bfloat16)
+    product = lax.dot_general(
+        weight_ref[...], scaled, (((0,), (0,)), ((), ())), preferred_element_type=jnp.float32
+    )
+    mixed[...] = product.reshape(mixed.shape).astype(mixed.dtype)
+    move.start(mixed, out_ref, sems[2:])
+    move.wait(mixed, out_ref, sems[2:])
+
+
+def mix_channels(collective_id, sums, weight):
+    move = Regular(("branch",), True)
+    groups, _, width = sums.shape
+    out = jax.ShapeDtypeStruct((groups, weight.shape[1] // groups, width), jnp.bfloat16)
+    vmem = pl.BlockSpec(memory_space=pltpu.VMEM)
+    return pl.pallas_call(
+        mix_kernel,
+        out_shape=out,
+        in_specs=[vmem, vmem],
+        out_specs=vmem,
+        scratch_shapes=[
+            pltpu.VMEM(sums.shape, sums.dtype),
+            pltpu.VMEM(out.shape, out.dtype),
+        ]
+        + move.semaphores()
+        + move.semaphores(),
+        compiler_params=pltpu.CompilerParams(
+            collective_id=collective_id, has_side_effects=True, vmem_limit_bytes=32 << 20
+        ),
+    )(sums, weight)
 
 
 def local(
@@ -99,12 +429,24 @@
     w_triangle_gate,
     w_triangle_out,
 ):
+    rows = lax.axis_size("row")
+    group_axes = ("branch", "row")
+    groups_all = group_size(group_axes)
+    seqs, residues, channels = alignment.shape
+    tile_first, tile_second, _ = pair_features.shape
     pair_normed = layer_norm(pair_features).astype(jnp.bfloat16)
     bias_tile = jnp.einsum(
         "ijc,ch->hij", pair_normed, w_bias, preferred_element_type=jnp.float32
     ).astype(jnp.bfloat16)
-    head_bias = lax.all_gather(bias_tile, "row", axis=2, tiled=True)
     row_normed = layer_norm(alignment).astype(jnp.bfloat16)
+    bias_slots, row_slots = exchange(
+        0,
+        [Regular(("row",), False), Regular(("col",), False)],
+        [bias_tile.reshape(HEAD_COUNT, -1), row_normed],
+    )
+    head_bias = jnp.transpose(
+        bias_slots.reshape(rows, HEAD_COUNT, tile_first, tile_second), (1, 2, 0, 3)
+    ).reshape(HEAD_COUNT, tile_first, rows * tile_second)
     local_weight = jnp.concatenate(
         [w_row[:, :ALIGN_CHANNELS], w_row[:, 3 * ALIGN_CHANNELS :]], axis=1
     )
@@ -113,7 +455,7 @@
         jnp.bfloat16
     )
     gate_values = jax.nn.sigmoid(local_projected[..., ALIGN_CHANNELS:])
-    gathered = lax.all_gather(row_normed, "col", axis=1, tiled=True)
+    gathered = jnp.transpose(row_slots, (1, 0, 2, 3)).reshape(seqs, -1, channels)
     key_value = project(gathered, w_row[:, ALIGN_CHANNELS : 3 * ALIGN_CHANNELS]).astype(
         jnp.bfloat16
     )
@@ -124,26 +466,38 @@
     alignment_row = (alignment.astype(jnp.float32) + project(row_gated, row_output_weight)).astype(
         jnp.bfloat16
     )
-    columns = lax.all_to_all(
-        alignment_row, ("branch", "row"), split_axis=1, concat_axis=0, tiled=True
-    )
+    part = residues // groups_all
+    outgoing = jnp.transpose(
+        alignment_row.reshape(seqs, groups_all, part, channels), (1, 0, 2, 3)
+    ).reshape(groups_all, seqs * part, channels)
+    (columns,) = exchange(1, [Regular(group_axes, True)], [outgoing])
+    columns = columns.reshape(groups_all * seqs, part, channels)
     column_new = column_attention(columns, w_column, column_output_weight)
-    alignment_out = lax.all_to_all(
-        column_new, ("branch", "row"), split_axis=0, concat_axis=1, tiled=True
-    )
-    outer_normed_input = layer_norm(alignment_out).astype(jnp.bfloat16)
+    outer_normed_input = layer_norm(column_new).astype(jnp.bfloat16)
     factor_pairs = project(outer_normed_input, outer_input_weight).astype(jnp.bfloat16)
-    left_factor = lax.all_gather(
-        factor_pairs[..., :FACTOR_CHANNELS], ("branch", "row"), axis=0, tiled=True
-    )
-    right_columns = lax.all_gather(factor_pairs[..., FACTOR_CHANNELS:], "col", axis=1, tiled=True)
-    right_rows = lax.all_to_all(right_columns, "row", split_axis=1, concat_axis=0, tiled=True)
-    right_factor = lax.all_gather(right_rows, "branch", axis=0, tiled=True)
+    all_seqs = groups_all * seqs
+    back, left_slots, right_slots = exchange(
+        2,
+        [Regular(group_axes, True), Regular(group_axes, False), ColToRow(True)],
+        [
+            column_new.reshape(groups_all, seqs * part, channels),
+            factor_pairs[..., :FACTOR_CHANNELS].reshape(all_seqs, part * FACTOR_CHANNELS),
+            factor_pairs[..., FACTOR_CHANNELS:].reshape(all_seqs, part * FACTOR_CHANNELS),
+        ],
+    )
+    alignment_out = jnp.transpose(
+        back.reshape(groups_all, seqs, part, channels), (1, 0, 2, 3)
+    ).reshape(seqs, residues, channels)
+    left_factor = jnp.transpose(left_slots, (1, 0, 2)).reshape(
+        all_seqs, residues, FACTOR_CHANNELS
+    )
+    right_factor = jnp.transpose(right_slots, (1, 0, 2)).reshape(
+        all_seqs, tile_second, FACTOR_CHANNELS
+    )
     outer_update = outer_mean(left_factor, right_factor, w_outer_out)
     pair_mid = (pair_features.astype(jnp.float32) + outer_update.astype(jnp.float32)).astype(
         jnp.bfloat16
     )
-    tile_first, tile_second, _ = pair_mid.shape
     groups = lax.axis_size("branch")
     branch_width = TRIANGLE_WIDTH // groups
     branch_start = lax.axis_index("branch") * branch_width
@@ -154,40 +508,32 @@
     w_in = lax.dynamic_slice_in_dim(
         w_triangle_in.reshape(PAIR_WIDTH, 4, TRIANGLE_WIDTH), branch_start, branch_width, 2
     )
-    w_in = w_in.reshape(PAIR_WIDTH, 4 * branch_width)
-    tri_projected = jnp.dot(flat_normed, w_in, preferred_element_type=jnp.float32)
-    tri_projected = tri_projected.reshape(tile_first, tile_second, 4, branch_width)
-    tri_left = (jax.nn.sigmoid(tri_projected[:, :, 1]) * tri_projected[:, :, 0]).astype(
-        jnp.bfloat16
-    )
-    tri_right = (jax.nn.sigmoid(tri_projected[:, :, 3]) * tri_projected[:, :, 2]).astype(
-        jnp.bfloat16
-    )
-    left_channels = jnp.transpose(tri_left, (2, 0, 1))
-    right_channels = jnp.transpose(tri_right, (2, 0, 1))
-    right_full = lax.all_gather(right_channels, "col", axis=1, tiled=True)
-    right_keys = lax.all_to_all(right_full, "row", split_axis=1, concat_axis=2, tiled=True)
+    gate_weight = lax.dynamic_slice_in_dim(w_triangle_gate, out_start, out_width, 1)
+    w_all = jnp.concatenate([w_in.reshape(PAIR_WIDTH, 4 * branch_width), gate_weight], axis=1)
+    projected = lax.dot_general(
+        w_all, flat_normed, (((0,), (1,)), ((), ())), preferred_element_type=jnp.float32
+    )
+    tri = projected[: 4 * branch_width].reshape(4, branch_width, -1)
+    tri_left = (jax.nn.sigmoid(tri[1]) * tri[0]).astype(jnp.bfloat16)
+    tri_right = (jax.nn.sigmoid(tri[3]) * tri[2]).astype(jnp.bfloat16)
+    output_gate = jax.nn.sigmoid(projected[4 * branch_width :])
+    per = rows // lax.axis_size("col")
+    right_parts = jnp.transpose(tri_right.reshape(branch_width, per, -1), (1, 0, 2))
+    left_slots, right_slots = exchange(
+        3, [Regular(("row",), False), ColToRow(False)], [tri_left, right_parts]
+    )
     product = jnp.einsum(
-        "cik,cjk->cij",
-        lax.all_gather(left_channels, "row", axis=2, tiled=True),
-        right_keys,
+        "rcik,rcjk->cij",
+        left_slots.reshape(rows, branch_width, tile_first, tile_second),
+        right_slots.reshape(rows, branch_width, tile_second, tile_second),
         preferred_element_type=jnp.float32,
-    )
-    triangle_sum = jnp.transpose(product, (1, 2, 0)).astype(jnp.bfloat16)
-    gate_weight = lax.dynamic_slice_in_dim(w_triangle_gate, out_start, out_width, 1)
-    output_gate = jax.nn.sigmoid(
-        jnp.dot(flat_normed, gate_weight, preferred_element_type=jnp.float32)
-    )
-    all_channels = lax.all_gather(triangle_sum, "branch", axis=2, tiled=True)
-    triangle_scaled = layer_norm(all_channels).astype(jnp.bfloat16)
-    column_weight = lax.dynamic_slice_in_dim(w_triangle_out, out_start, out_width, 1)
-    mixed_channels = jnp.dot(
-        triangle_scaled.reshape(-1, TRIANGLE_WIDTH),
-        column_weight,
-        preferred_element_type=jnp.float32,
-    )
+    ).astype(jnp.bfloat16)
+    sums = jnp.transpose(product.reshape(branch_width, groups, -1), (1, 0, 2))
+    mixed = mix_channels(4, sums, w_triangle_out)
+    mixed = jnp.transpose(mixed, (1, 0, 2)).reshape(out_width, -1)
+    update = jnp.transpose(output_gate * mixed.astype(jnp.float32))
     pair_slice = lax.dynamic_slice_in_dim(pair_mid, out_start, out_width, 2).reshape(-1, out_width)
-    pair_out = (pair_slice.astype(jnp.float32) + output_gate * mixed_channels).astype(jnp.bfloat16)
+    pair_out = (pair_slice.astype(jnp.float32) + update).astype(jnp.bfloat16)
     return (alignment_out, pair_out.reshape(tile_first, tile_second, out_width))
 
 

time: 212 us -> 120 us (0.57)
  blocking collectives: 133 us -> 0 us
  Pallas kernels: 0 us -> 60.8 us
  starting transfers between devices: 10.2 us -> 0 us
  waiting for transfers between devices: 7.47 us -> 0 us
    all_gather x8 -> x0, blocking collectives: 119 us -> none  [the longest x1 42.2 us: local(): lax.all_gather(factor_pairs[..., :FACTOR_CHANNELS], ('branch', 'row'), ax...]
    pallas_call x0 -> x5, Pallas kernels: none -> 60.8 us  [the longest x4 48 us: exchange(): pl.pallas_call(functools.partial(exchange_kernel, moves), out_shape=[jax....]
    all_to_all x1 -> x0, blocking collectives: 13.5 us -> none  [local(): lax.all_to_all(alignment_row, ('branch', 'row'), split_axis=1, concat_axi...]
    reshape x1 -> x14, local copies, waits for them, and re-layouts: 0.04 us -> 10.9 us  [the longest x1 2.8 us: local(): left_slots.reshape(rows, branch_width, tile_first, tile_second)]
    all_to_all x3 -> x0, starting transfers between devices: 10.2 us -> none  [the longest x1 3.51 us: local(): lax.all_to_all(column_new, ('branch', 'row'), split_axis=0, concat_axis=1...]
    all_to_all x3 -> x0, waiting for transfers between devices: 7.47 us -> none  [the longest x1 7.46 us: local(): lax.all_to_all(column_new, ('branch', 'row'), split_axis=0, concat_axis=1...]
    all_gather x3 -> x0, local copies, waits for them, and re-layouts: 5.64 us -> none  [the longest x1 3.89 us: local(): lax.all_gather(left_channels, 'row', axis=2, tiled=True)]
    all_to_all x5 -> x0, local copies, waits for them, and re-layouts: 3.94 us -> none  [the longest x2 3.8 us: local(): lax.all_to_all(right_full, 'row', split_axis=1, concat_axis=2, tiled=True)]
  transfers between devices with their start and end apart: 3 -> 0, of which waited for: 1 -> 0; matrix products, arithmetic and copies ran while one was open for 4% -> 0% of each run, Pallas kernels for 0% -> 0%
where the time goes in v1:
time: 120 us; the launch traced here: 119 us
  Pallas kernels  60.8 us (51%)
  local copies, waits for them, and re-layouts  29.9 us (25%)
  matrix products  20.4 us (17%)
  other arithmetic  6.81 us (6%)
  between operations  1.3 us (1%)
    pallas_call x4, Pallas kernels, exchange(): pl.pallas_call(functools.partial(exchange_kernel, moves), out_shape=[jax....  48 us
    pallas_call x1, Pallas kernels, mix_channels(): pl.pallas_call(mix_kernel, out_shape=out, in_specs=[vmem, vmem], out_spec...  12.8 us
    dot_general x1, matrix products, attend(): jnp.einsum('bhqk,bkhd->bqhd', attention, value_heads, preferred_element_t...  5.46 us
    unnamed x40, local copies, waits for them, and re-layouts  5.01 us
    reshape x1, local copies, waits for them, and re-layouts, local(): left_slots.reshape(rows, branch_width, tile_first, tile_second)  2.8 us
    dot_general x6, matrix products, project(): jnp.dot(flat_rows, weight_matrix, preferred_element_type=jnp.float32)  2.63 us

profile of v1, /device:TPU:0, one launch (start us, length us, event | category | flops | bytes accessed | tf_op | source)
XLA Modules:
  0.0 119.2 jit_solution(9585192674480933742)
XLA Ops:
  0.7 1.8 %copy.112 = bf16[64,32,128]{0,2,1:T(8,128)(2,1)S(1)} copy(bf16[64,32,128]{2,1,0:T(8,128)(2,1)} %param.13) | data formatting | bytes 1048576 | tf_op args[1]
  5.6 10.1 %shard_map.131 = (bf16[4,8,2048]{2,1,0:T(8,128)(2,1)}, bf16[2,4,64,256]{3,2,1,0:T(8,128)(2,1)}) custom-call(bf16[8,2048]{1,0:T(8,128)(2,1)} %reshape.241.refs_0_, bf16[4,64,256]{2,1,0:T(8,128)(2,1)} %fusion.32.refs_1_), custom_call_target="tpu_custom_call" | custom-call | tf_op jit(solution)/shard_map/pallas_call | solution.py:366
  15.6 1.0 copy.115
  17.0 0.8 copy.116
  19.1 0.8 copy.118
  20.8 1.8 %fusion.97 = f32[4,8,64]{2,1,0:T(8,128)S(1)} fusion(bf16[4,64,8,32]{1,3,2,0:T(8,128)(2,1)S(1)} %bitcast.124, bf16[4,128,8,32]{1,3,2,0:T(8,128)(2,1)} %bitcast.126, f32[8,64,128]{2,1,0:T(8,128)S(1)} %copy.120), kind=kOutput, calls=%fused_computation.142 | convolution fusion | flops 17563776 | bytes 663552 | tf_op jit(solution)/shard_map/sub | solution.py:52
  23.0 5.5 %fusion.25 = f32[4,8,32,64]{3,2,1,0:T(8,128)} fusion(bf16[4,128,8,32]{1,3,2,0:T(8,128)(2,1)} %bitcast.143, f32[4,8,64]{2,1,0:T(8,128)S(1)} %fusion.97, f32[4,8,64,128]{3,2,1,0:T(8,128)S(1)} %convolution_add_fusion), kind=kOutput, calls=%fused_computation.40 | convolution fusion | flops 17565824 | bytes 1581056 | tf_op jit(solution)/shard_map/bhqk,bkhd->bqhd/dot_general | solution.py:58
  28.4 1.2 %copy.121 = f32[4,64,256]{2,1,0:T(8,128)S(1)} copy(f32[4,64,256]{1,2,0:T(8,128)} %bitcast.136) | data formatting | bytes 524288 | tf_op jit(solution)/shard_map/reshape | solution.py:61
  30.7 8.9 %shard_map.132 = bf16[16,16,256]{2,1,0:T(8,128)(2,1)} custom-call(bf16[16,16,256]{2,1,0:T(8,128)(2,1)} %reshape.247.refs_0_), custom_call_target="tpu_custom_call" | custom-call | tf_op jit(solution)/shard_map/pallas_call | solution.py:366
  39.6 1.0 reshape.267
  40.6 1.0 convert_reduce_fusion.4
  41.6 1.1 multiply_reduce_fusion
  43.4 0.8 copy.126
  45.1 1.3 %fusion.100 = f32[4,8,64,64]{2,3,1,0:T(8,128)} fusion(bf16[64,4,8,32]{0,3,2,1:T(8,128)(2,1)S(1)} %bitcast.131, bf16[64,4,8,32]{0,3,2,1:T(8,128)(2,1)S(1)} %bitcast.133), kind=kOutput, calls=%fused_computation.145 | convolution fusion | flops 8388608 | bytes 786432 | tf_op jit(solution)/shard_map/qbhd,kbhd->bhqk/dot_general | solution.py:43
  46.5 2.0 %fusion.26 = f32[4,8,32,64]{3,2,1,0:T(8,128)S(1)} fusion(bf16[64,4,8,32]{0,3,2,1:T(8,128)(2,1)} %bitcast.142, f32[4,8,64]{2,1,0:T(8,128)S(1)} %fusion.99, f32[4,8,64,64]{2,3,1,0:T(8,128)} %fusion.100), kind=kOutput, calls=%fused_computation.41 | convolution fusion | flops 8783935 | bytes 925696 | tf_op jit(solution)/shard_map/bhqk,kbhd->qbhd/dot_general | solution.py:54
  48.5 0.9 copy.130
  49.4 1.2 %convert_reduce_fusion.3 = (f32[64,4]{0,1:T(4,128)S(1)}, bf16[64,4,256]{2,0,1:T(8,128)(2,1)S(1)}) fusion(bf16[256,256]{1,0:T(8,128)(2,1)S(1)} %copy-done.15, f32[64,4,256]{2,0,1:T(8,128)} %copy.130, f32[64,4,1024]{2,0,1:T(8,128)S(1)} %get-tuple-element.35, f32[64,4,256]{2,1,0:T(4,128)S(1)} %reshape.267), kind=kOutput, calls=%fused_computation.45 | convolution fusion | flops 34144000 | bytes 1049600 | tf_op jit(solution)/shard_map/dot_general | solution.py:30
  53.3 13.8 %shard_map.133 = (bf16[16,16,256]{2,1,0:T(8,128)(2,1)}, bf16[16,64,128]{2,1,0:T(8,128)(2,1)}, bf16[8,64,128]{2,1,0:T(8,128)(2,1)}) custom-call(bf16[16,16,256]{2,1,0:T(8,128)(2,1)} %reshape.252.refs_0_, bf16[64,128]{1,0:T(8,128)(2,1)} %copy.133.refs_1_, bf16[64,128]{1,0:T(8,128)(2,1)} %copy.134.refs_2_), custom_call_target="tpu_custom_call" | custom-call | tf_op jit(solution)/shard_map/pallas_call | solution.py:366
  67.1 0.9 reshape.255
  68.8 1.1 copy.136
  69.9 1.2 %copy.137 = bf16[64,16,128]{0,2,1:T(8,128)(2,1)S(1)} copy(bf16[64,16,128]{2,0,1:T(8,128)(2,1)} %bitcast.141) | data formatting | bytes 524288 | tf_op jit(solution)/shard_map/transpose | solution.py:491
  71.8 2.3 %multiply_convert_fusion = bf16[32,32,64,32]{2,1,3,0:T(8,128)(2,1)S(1)} fusion(bf16[64,32,32,1]{0,2,3,1:T(8,128)(2,1)S(1)} %bitcast.128, bf16[64,64,32]{1,0,2:T(8,128)(2,1)S(1)} %copy.138), kind=kOutput, calls=%fused_computation.2 | convolution fusion | flops 272629760 | bytes 4587520 | tf_op jit(solution)/shard_map/sic,sje->ijce/dot_general | solution.py:84
  74.1 1.4 %convert_reduce_fusion.1 = (f32[64,32]{0,1:T(8,128)S(1)}, bf16[64,32,128]{0,2,1:T(8,128)(2,1)S(1)}) fusion(bf16[64,32,1024]{0,2,1:T(8,128)(2,1)S(1)} %bitcast.119, bf16[1024,128]{1,0:T(8,128)(2,1)S(1)} %copy-done.13, bf16[64,32,128]{0,2,1:T(8,128)(2,1)S(1)} %copy.112), kind=kOutput, calls=%fused_computation.7 | convolution fusion | flops 538703872 | bytes 5513216 | tf_op jit(solution)/shard_map/dot_general | solution.py:88
  77.4 0.8 copy.144
  78.9 1.1 copy-done.2
  81.4 15.2 %shard_map.134 = (bf16[4,32,2048]{2,1,0:T(8,128)(2,1)}, bf16[4,32,1024]{2,1,0:T(8,128)(2,1)}) custom-call(bf16[32,2048]{1,0:T(8,128)(2,1)} %get-tuple-element.25.refs_0_, bf16[2,32,1024]{2,1,0:T(8,128)(2,1)} %bitcast.138), custom_call_target="tpu_custom_call" | custom-call | tf_op jit(solution)/shard_map/pallas_call | solution.py:366
  96.6 2.8 %reshape.262 = bf16[4,32,64,32]{3,2,1,0:T(8,128)(2,1)S(1)} reshape(bf16[4,32,2048]{2,1,0:T(8,128)(2,1)} %get-tuple-element.14) | data formatting | bytes 1048576 | tf_op jit(solution)/shard_map/reshape | solution.py:527
  99.4 1.8 %reshape.263 = bf16[4,32,32,32]{3,2,1,0:T(8,128)(2,1)} reshape(bf16[4,32,1024]{2,1,0:T(8,128)(2,1)S(1)} %copy-done.9) | data formatting | bytes 524288 | tf_op jit(solution)/shard_map/reshape | solution.py:528
  101.2 1.9 %fusion.15 = bf16[32,64,32]{1,2,0:T(8,128)(2,1)S(1)} fusion(bf16[4,32,64,32]{3,2,1,0:T(8,128)(2,1)S(1)} %reshape.262, bf16[4,32,32,32]{3,2,1,0:T(8,128)(2,1)} %reshape.263), kind=kOutput, calls=%fused_computation.25 | convolution fusion | flops 16842752 | bytes 917504 | tf_op jit(solution)/shard_map/rcik,rcjk->cij/dot_general | solution.py:525
  103.8 12.8 %shard_map.135 = bf16[4,32,512]{2,1,0:T(8,128)(2,1)S(1)} custom-call(bf16[4,32,512]{2,1,0:T(8,128)(2,1)S(1)} %bitcast.118, bf16[128,128]{1,0:T(8,128)(2,1)S(1)} %copy-done.1), custom_call_target="tpu_custom_call" | custom-call | tf_op jit(solution)/shard_map/pallas_call | solution.py:401
  116.7 1.0 fusion.67
  118.1 1.1 copy.150
  (105 shorter events, 17.4 us)
Async XLA Ops:
  0.6 42.4 %copy-start = (bf16[256,1024]{1,0:T(8,128)(2,1)S(1)}, bf16[256,1024]{1,0:T(8,128)(2,1)}, u32[]{:S(2)}) copy-start(bf16[256,1024]{1,0:T(8,128)(2,1)} %param.17) | copy-start | bytes 1572868
  0.6 2.5 %copy-start.17 = (bf16[128,8]{0,1:T(8,128)(2,1)S(1)}, bf16[128,8]{0,1:T(8,128)(2,1)}, u32[]{:S(2)}) copy-start(bf16[128,8]{0,1:T(8,128)(2,1)} %param.16) | copy-start | bytes 6148
  2.4 2.0 %copy-start.6 = (bf16[4,64,256]{2,1,0:T(8,128)(2,1)S(1)}, bf16[4,64,256]{2,1,0:T(8,128)(2,1)}, u32[]{:S(2)}) copy-start(bf16[4,64,256]{2,1,0:T(8,128)(2,1)} %param.12) | copy-start | bytes 393220
  2.7 13.9 %copy-start.8 = (bf16[256,1024]{1,0:T(8,128)(2,1)S(1)}, bf16[256,1024]{1,0:T(8,128)(2,1)}, u32[]{:S(2)}) copy-start(bf16[256,1024]{1,0:T(8,128)(2,1)} %param.14) | copy-start | bytes 1572868
  5.6 12.3 %copy-start.5 = (bf16[4,64,256]{2,1,0:T(8,128)(2,1)S(1)}, bf16[4,64,256]{2,1,0:T(8,128)(2,1)}, u32[]{:S(2)}) copy-start(bf16[4,64,256]{2,1,0:T(8,128)(2,1)} %fusion.32.refs_1_) | copy-start | bytes 393220
  16.9 3.0 %copy-start.10 = (bf16[4,8,2048]{2,1,0:T(8,128)(2,1)S(1)}, bf16[4,8,2048]{2,1,0:T(8,128)(2,1)}, u32[]{:S(2)}) copy-start(bf16[4,8,2048]{2,1,0:T(8,128)(2,1)} %get-tuple-element.10) | copy-start | bytes 393220
  18.1 0.8 copy-start.3
  20.6 2.0 %copy-start.7 = (bf16[4,128,256]{1,2,0:T(8,128)(2,1)S(1)}, bf16[4,128,256]{1,2,0:T(8,128)(2,1)}, u32[]{:S(2)}) copy-start(bf16[4,128,256]{1,2,0:T(8,128)(2,1)} %copy.118) | copy-start | bytes 786436
  22.9 6.7 %copy-start.4 = (f32[4,64,512]{2,1,0:T(8,128)S(1)}, f32[4,64,512]{2,1,0:T(8,128)}, u32[]{:S(2)}) copy-start(f32[4,64,512]{2,1,0:T(8,128)} %copy-done.3) | copy-start | bytes 1572868
  22.9 6.7 %copy-start.14 = (bf16[256,256]{1,0:T(8,128)(2,1)S(1)}, bf16[256,256]{1,0:T(8,128)(2,1)}, u32[]{:S(2)}) copy-start(bf16[256,256]{1,0:T(8,128)(2,1)} %param.15) | copy-start | bytes 393220
  46.5 2.9 %copy-start.15 = (bf16[256,256]{1,0:T(8,128)(2,1)S(1)}, bf16[256,256]{1,0:T(8,128)(2,1)}, u32[]{:S(2)}) copy-start(bf16[256,256]{1,0:T(8,128)(2,1)} %param.18) | copy-start | bytes 393220
  49.4 2.3 %copy-start.16 = (bf16[256,64]{0,1:T(8,128)(2,1)S(1)}, bf16[256,64]{0,1:T(8,128)(2,1)}, u32[]{:S(2)}) copy-start(bf16[256,64]{0,1:T(8,128)(2,1)} %param.19) | copy-start | bytes 98308
  71.7 2.3 %copy-start.13 = (bf16[1024,128]{1,0:T(8,128)(2,1)S(1)}, bf16[1024,128]{1,0:T(8,128)(2,1)}, u32[]{:S(2)}) copy-start(bf16[1024,128]{1,0:T(8,128)(2,1)} %param.20) | copy-start | bytes 786436
  76.9 1.3 %copy-start.12 = (bf16[128,128]{1,0:T(8,128)(2,1)S(1)}, bf16[128,128]{1,0:T(8,128)(2,1)}, u32[]{:S(2)}) copy-start(bf16[128,128]{1,0:T(8,128)(2,1)} %param.22) | copy-start | bytes 98308
  76.9 1.4 %copy-start.11 = (bf16[128,512]{1,0:T(8,128)(2,1)S(1)}, bf16[128,512]{1,0:T(8,128)(2,1)}, u32[]{:S(2)}) copy-start(bf16[128,512]{1,0:T(8,128)(2,1)} %param.21) | copy-start | bytes 393220
  78.9 1.1 copy-start.2
  96.6 2.8 %copy-start.9 = (bf16[4,32,1024]{2,1,0:T(8,128)(2,1)S(1)}, bf16[4,32,1024]{2,1,0:T(8,128)(2,1)}, u32[]{:S(2)}) copy-start(bf16[4,32,1024]{2,1,0:T(8,128)(2,1)} %get-tuple-element.15) | copy-start | bytes 786436
  101.2 2.6 %copy-start.1 = (bf16[128,128]{1,0:T(8,128)(2,1)S(1)}, bf16[128,128]{1,0:T(8,128)(2,1)}, u32[]{:S(2)}) copy-start(bf16[128,128]{1,0:T(8,128)(2,1)} %weight_ref.1) | copy-start | bytes 98308

commit v2 on v1

--- a/solution.py
+++ b/solution.py
@@ -2,6 +2,7 @@
 
 import jax
 import jax.numpy as jnp
+import numpy as np
 from jax import lax
 from jax.experimental import pallas as pl
 from jax.experimental.pallas import tpu as pltpu
@@ -415,6 +416,259 @@
     )(sums, weight)
 
 
+def softmax_down(scores):
+    peak = jnp.max(scores, axis=0, keepdims=True)
+    powers = jnp.exp(scores - peak)
+    return (powers / jnp.sum(powers, axis=0, keepdims=True)).astype(jnp.bfloat16)
+
+
+def dot(a, b, a_dim=1, b_dim=0):
+    return lax.dot_general(
+        a, b, (((a_dim,), (b_dim,)), ((), ())), preferred_element_type=jnp.float32
+    )
+
+
+def align_kernel(
+    seqs,
+    part,
+    align_ref,
+    bias_ref,
+    w_row_ref,
+    row_out_ref,
+    w_col_ref,
+    col_out_ref,
+    w_left_ref,
+    w_right_ref,
+    permute_ref,
+    same_ref,
+    out_ref,
+    left_slots,
+    right_slots,
+    normed,
+    bias_slots,
+    gathered,
+    outgoing,
+    columns,
+    col_new,
+    back,
+    normed_cols,
+    left,
+    right,
+    *sems,
+):
+    bf16, width = jnp.bfloat16, ALIGN_CHANNELS
+    group_axes = ("branch", "row")
+    groups = group_size(group_axes)
+    over_row, over_col = Regular(("row",), False), Regular(("col",), False)
+    swap, spread, aim = Regular(group_axes, True), Regular(group_axes, False), ColToRow(True)
+    total = swap.greet() + over_col.greet() + aim.greet()
+    pl.semaphore_wait(pltpu.get_barrier_semaphore(), total)
+    over_row.start(bias_ref, bias_slots, sems[0:2])
+    normed[...] = layer_norm(align_ref[...]).astype(bf16)
+    over_col.start(normed, gathered, sems[2:4])
+    residues = align_ref.shape[0] // seqs
+    lanes = lax.broadcasted_iota(jnp.int32, (residues, width), 1)
+    picks = [
+        (lanes >= h * HEAD_CHANNELS) & (lanes < (h + 1) * HEAD_CHANNELS) for h in range(HEAD_COUNT)
+    ]
+    query = dot(normed[...], w_row_ref[:, :width]) * HEAD_CHANNELS ** (-0.5)
+    gate = jax.nn.sigmoid(dot(normed[...], w_row_ref[:, 3 * width :]))
+    over_col.wait(normed, gathered, sems[2:4])
+    cols = gathered.shape[0]
+    key_value = [
+        dot(gathered[q], w_row_ref[:, width : 3 * width]).astype(bf16) for q in range(cols)
+    ]
+    over_row.wait(bias_ref, bias_slots, sems[0:2])
+    bias = bias_slots[...].astype(jnp.float32).reshape(-1, bias_ref.shape[1])
+    mixed = []
+    for s in range(seqs):
+        own = slice(s * residues, (s + 1) * residues)
+        key = jnp.concatenate([kv[own, :width] for kv in key_value], axis=0)
+        value = jnp.concatenate([kv[own, width:] for kv in key_value], axis=0)
+        heads = jnp.concatenate([jnp.where(p, query[own], 0.0) for p in picks], axis=0)
+        weights = softmax_down(dot(key, heads.astype(bf16), 1, 1) + bias)
+        spreadout = dot(weights, value, 0, 0)
+        attended = jnp.zeros((residues, width), jnp.float32)
+        for h, p in enumerate(picks):
+            attended = jnp.where(p, spreadout[h * residues : (h + 1) * residues], attended)
+        mixed.append(attended)
+    row_gated = (gate * jnp.concatenate(mixed, axis=0)).astype(bf16)
+    updated = align_ref[...].astype(jnp.float32) + dot(row_gated, row_out_ref[...])
+    outgoing[...] = dot(permute_ref[...], updated.astype(bf16)).astype(bf16).reshape(outgoing.shape)
+    swap.start(outgoing, columns, sems[4:6])
+    swap.wait(outgoing, columns, sems[4:6])
+    entries = columns[...].reshape(-1, width)
+    count = entries.shape[0]
+    col_normed = layer_norm(entries).astype(bf16)
+    projected = dot(col_normed, w_col_ref[...])
+    query = projected[:, :width] * HEAD_CHANNELS ** (-0.5)
+    key = projected[:, width : 2 * width].astype(bf16)
+    value = projected[:, 2 * width : 3 * width].astype(bf16)
+    gate = jax.nn.sigmoid(projected[:, 3 * width :])
+    same = same_ref[...].astype(jnp.float32) > 0.5
+    lanes = lax.broadcasted_iota(jnp.int32, (count, width), 1)
+    attended = jnp.zeros((count, width), jnp.float32)
+    for h in range(HEAD_COUNT):
+        pick = (lanes >= h * HEAD_CHANNELS) & (lanes < (h + 1) * HEAD_CHANNELS)
+        scores = dot(key, jnp.where(pick, query, 0.0).astype(bf16), 1, 1)
+        weights = softmax_down(jnp.where(same, scores, jnp.finfo(jnp.float32).min))
+        attended = jnp.where(pick, dot(weights, value, 0, 0), attended)
+    col_gated = (gate * attended).astype(bf16)
+    new = (entries.astype(jnp.float32) + dot(col_gated, col_out_ref[...])).astype(bf16)
+    normed_new = layer_norm(new)
+    for half in range(width // 128):
+        normed_cols[half] = normed_new[:, half * 128 : (half + 1) * 128]
+    all_seqs = count // part
+    left_sum = right_sum = None
+    for r in range(part):
+        rows_r = jnp.concatenate(
+            [normed_cols[half, pl.ds(r, all_seqs, stride=part), :] for half in range(width // 128)],
+            axis=1,
+        ).astype(bf16)
+        left_r, right_r = dot(rows_r, w_left_ref[r]), dot(rows_r, w_right_ref[r])
+        left_sum = left_r if r == 0 else left_sum + left_r
+        right_sum = right_r if r == 0 else right_sum + right_r
+    left[...] = left_sum.astype(bf16)
+    right[...] = right_sum.astype(bf16)
+    aim.start(right, right_slots, sems[10:13])
+    spread.start(left, left_slots, sems[8:10])
+    col_new[...] = new.reshape(col_new.shape)
+    swap.start(col_new, back, sems[6:8])
+    swap.wait(col_new, back, sems[6:8])
+    result = dot(permute_ref[...], back[...].reshape(-1, width), 0, 0)
+    out_ref[...] = result.astype(bf16)
+    aim.wait(right, right_slots, sems[10:13])
+    spread.wait(left, left_slots, sems[8:10])
+
+
+def align_update(collective_id, alignment, bias, w_row, row_out, w_col, col_out, w_factor):
+    bf16 = jnp.bfloat16
+    seqs, residues, width = alignment.shape
+    group_axes = ("branch", "row")
+    groups = group_size(group_axes)
+    part = residues // groups
+    count = seqs * residues
+    place = np.arange(count).reshape(seqs, groups, part).transpose(1, 0, 2).reshape(-1)
+    permute = jnp.asarray(np.eye(count, dtype=np.float32)[place], bf16)
+    rest = np.arange(count) % part
+    same = jnp.asarray((rest[:, None] == rest[None, :]).astype(np.float32), bf16)
+    eye = jnp.asarray(np.eye(part, dtype=np.float32), bf16)
+    spread_out = lambda w: (eye[:, None, :, None] * w[None, :, None, :]).reshape(part, width, -1)
+    w_left = spread_out(w_factor[:, :FACTOR_CHANNELS])
+    w_right = spread_out(w_factor[:, FACTOR_CHANNELS:])
+    over_row, over_col = Regular(("row",), False), Regular(("col",), False)
+    swap, spread, aim = Regular(group_axes, True), Regular(group_axes, False), ColToRow(True)
+    factor = jax.ShapeDtypeStruct((groups * seqs, part * FACTOR_CHANNELS), bf16)
+    slots = (groups, seqs * part, width)
+    scratch = [
+        pltpu.VMEM((count, width), bf16),
+        pltpu.VMEM((lax.axis_size("row"),) + bias.shape, bf16),
+        pltpu.VMEM((lax.axis_size("col"), count, width), bf16),
+        pltpu.VMEM(slots, bf16),
+        pltpu.VMEM(slots, bf16),
+        pltpu.VMEM(slots, bf16),
+        pltpu.VMEM(slots, bf16),
+        pltpu.VMEM((width // 128, count, 128), jnp.float32),
+        pltpu.VMEM(factor.shape, bf16),
+        pltpu.VMEM(factor.shape, bf16),
+    ]
+    for move in (over_row, over_col, swap, swap, spread, aim):
+        scratch += move.semaphores()
+    vmem = pl.BlockSpec(memory_space=pltpu.VMEM)
+    anywhere = pl.BlockSpec(memory_space=pl.ANY)
+    out, left_slots, right_slots = pl.pallas_call(
+        functools.partial(align_kernel, seqs, part),
+        out_shape=[
+            jax.ShapeDtypeStruct((count, width), bf16),
+            spread.slots(factor),
+            aim.slots(factor),
+        ],
+        in_specs=[vmem] * 10,
+        out_specs=[vmem, anywhere, anywhere],
+        scratch_shapes=scratch,
+        compiler_params=pltpu.CompilerParams(
+            collective_id=collective_id, has_side_effects=True, vmem_limit_bytes=48 << 20
+        ),
+    )(
+        alignment.reshape(count, width),
+        bias,
+        w_row,
+        row_out,
+        w_col,
+        col_out,
+        w_left,
+        w_right,
+        permute,
+        same,
+    )
+    return out.reshape(alignment.shape), left_slots, right_slots
+
+
+def align_unfused(
+    alignment, pair_normed, w_row, row_output_weight, w_bias, w_column, column_output_weight,
+    outer_input_weight,
+):
+    rows = lax.axis_size("row")
+    group_axes = ("branch", "row")
+    groups_all = group_size(group_axes)
+    seqs, residues, channels = alignment.shape
+    tile_first, tile_second, _ = pair_normed.shape
+    bias_tile = jnp.einsum(
+        "ijc,ch->hij", pair_normed, w_bias, preferred_element_type=jnp.float32
+    ).astype(jnp.bfloat16)
+    row_normed = layer_norm(alignment).astype(jnp.bfloat16)
+    bias_slots, row_slots = exchange(
+        0,
+        [Regular(("row",), False), Regular(("col",), False)],
+        [bias_tile.reshape(HEAD_COUNT, -1), row_normed],
+    )
+    head_bias = jnp.transpose(
+        bias_slots.reshape(rows, HEAD_COUNT, tile_first, tile_second), (1, 2, 0, 3)
+    ).reshape(HEAD_COUNT, tile_first, rows * tile_second)
+    local_weight = jnp.concatenate(
+        [w_row[:, :ALIGN_CHANNELS], w_row[:, 3 * ALIGN_CHANNELS :]], axis=1
+    )
+    local_projected = project(row_normed, local_weight)
+    query_matrix = (local_projected[..., :ALIGN_CHANNELS] * HEAD_CHANNELS ** (-0.5)).astype(
+        jnp.bfloat16
+    )
+    gate_values = jax.nn.sigmoid(local_projected[..., ALIGN_CHANNELS:])
+    gathered = jnp.transpose(row_slots, (1, 0, 2, 3)).reshape(seqs, -1, channels)
+    key_value = project(gathered, w_row[:, ALIGN_CHANNELS : 3 * ALIGN_CHANNELS]).astype(
+        jnp.bfloat16
+    )
+    key_matrix = key_value[..., :ALIGN_CHANNELS]
+    value_matrix = key_value[..., ALIGN_CHANNELS:]
+    attended = attend(query_matrix, key_matrix, value_matrix, head_bias, False)
+    row_gated = (gate_values * attended).astype(jnp.bfloat16)
+    alignment_row = (alignment.astype(jnp.float32) + project(row_gated, row_output_weight)).astype(
+        jnp.bfloat16
+    )
+    part = residues // groups_all
+    outgoing = jnp.transpose(
+        alignment_row.reshape(seqs, groups_all, part, channels), (1, 0, 2, 3)
+    ).reshape(groups_all, seqs * part, channels)
+    (columns,) = exchange(1, [Regular(group_axes, True)], [outgoing])
+    columns = columns.reshape(groups_all * seqs, part, channels)
+    column_new = column_attention(columns, w_column, column_output_weight)
+    outer_normed_input = layer_norm(column_new).astype(jnp.bfloat16)
+    factor_pairs = project(outer_normed_input, outer_input_weight).astype(jnp.bfloat16)
+    all_seqs = groups_all * seqs
+    back, left_slots, right_slots = exchange(
+        2,
+        [Regular(group_axes, True), Regular(group_axes, False), ColToRow(True)],
+        [
+            column_new.reshape(groups_all, seqs * part, channels),
+            factor_pairs[..., :FACTOR_CHANNELS].reshape(all_seqs, part * FACTOR_CHANNELS),
+            factor_pairs[..., FACTOR_CHANNELS:].reshape(all_seqs, part * FACTOR_CHANNELS),
+        ],
+    )
+    alignment_out = jnp.transpose(
+        back.reshape(groups_all, seqs, part, channels), (1, 0, 2, 3)
+    ).reshape(seqs, residues, channels)
+    return alignment_out, left_slots, right_slots
+
+
 def local(
     alignment,
     pair_features,
@@ -435,59 +689,32 @@
     seqs, residues, channels = alignment.shape
     tile_first, tile_second, _ = pair_features.shape
     pair_normed = layer_norm(pair_features).astype(jnp.bfloat16)
-    bias_tile = jnp.einsum(
-        "ijc,ch->hij", pair_normed, w_bias, preferred_element_type=jnp.float32
-    ).astype(jnp.bfloat16)
-    row_normed = layer_norm(alignment).astype(jnp.bfloat16)
-    bias_slots, row_slots = exchange(
-        0,
-        [Regular(("row",), False), Regular(("col",), False)],
-        [bias_tile.reshape(HEAD_COUNT, -1), row_normed],
-    )
-    head_bias = jnp.transpose(
-        bias_slots.reshape(rows, HEAD_COUNT, tile_first, tile_second), (1, 2, 0, 3)
-    ).reshape(HEAD_COUNT, tile_first, rows * tile_second)
-    local_weight = jnp.concatenate(
-        [w_row[:, :ALIGN_CHANNELS], w_row[:, 3 * ALIGN_CHANNELS :]], axis=1
-    )
-    local_projected = project(row_normed, local_weight)
-    query_matrix = (local_projected[..., :ALIGN_CHANNELS] * HEAD_CHANNELS ** (-0.5)).astype(
-        jnp.bfloat16
-    )
-    gate_values = jax.nn.sigmoid(local_projected[..., ALIGN_CHANNELS:])
-    gathered = jnp.transpose(row_slots, (1, 0, 2, 3)).reshape(seqs, -1, channels)
-    key_value = project(gathered, w_row[:, ALIGN_CHANNELS : 3 * ALIGN_CHANNELS]).astype(
-        jnp.bfloat16
-    )
-    key_matrix = key_value[..., :ALIGN_CHANNELS]
-    value_matrix = key_value[..., ALIGN_CHANNELS:]
-    attended = attend(query_matrix, key_matrix, value_matrix, head_bias, False)
-    row_gated = (gate_values * attended).astype(jnp.bfloat16)
-    alignment_row = (alignment.astype(jnp.float32) + project(row_gated, row_output_weight)).astype(
-        jnp.bfloat16
-    )
-    part = residues // groups_all
-    outgoing = jnp.transpose(
-        alignment_row.reshape(seqs, groups_all, part, channels), (1, 0, 2, 3)
-    ).reshape(groups_all, seqs * part, channels)
-    (columns,) = exchange(1, [Regular(group_axes, True)], [outgoing])
-    columns = columns.reshape(groups_all * seqs, part, channels)
-    column_new = column_attention(columns, w_column, column_output_weight)
-    outer_normed_input = layer_norm(column_new).astype(jnp.bfloat16)
-    factor_pairs = project(outer_normed_input, outer_input_weight).astype(jnp.bfloat16)
+    if (seqs * residues // groups_all) % 16 == 0 and residues % 16 == 0:
+        bias = jnp.einsum(
+            "ijc,ch->jhi", pair_normed, w_bias, preferred_element_type=jnp.float32
+        ).astype(jnp.bfloat16)
+        alignment_out, left_slots, right_slots = align_update(
+            5,
+            alignment,
+            bias.reshape(tile_second, -1),
+            w_row,
+            row_output_weight,
+            w_column,
+            column_output_weight,
+            outer_input_weight,
+        )
+    else:
+        alignment_out, left_slots, right_slots = align_unfused(
+            alignment,
+            pair_normed,
+            w_row,
+            row_output_weight,
+            w_bias,
+            w_column,
+            column_output_weight,
+            outer_input_weight,
+        )
     all_seqs = groups_all * seqs
-    back, left_slots, right_slots = exchange(
-        2,
-        [Regular(group_axes, True), Regular(group_axes, False), ColToRow(True)],
-        [
-            column_new.reshape(groups_all, seqs * part, channels),
-            factor_pairs[..., :FACTOR_CHANNELS].reshape(all_seqs, part * FACTOR_CHANNELS),
-            factor_pairs[..., FACTOR_CHANNELS:].reshape(all_seqs, part * FACTOR_CHANNELS),
-        ],
-    )
-    alignment_out = jnp.transpose(
-        back.reshape(groups_all, seqs, part, channels), (1, 0, 2, 3)
-    ).reshape(seqs, residues, channels)
     left_factor = jnp.transpose(left_slots, (1, 0, 2)).reshape(
         all_seqs, residues, FACTOR_CHANNELS
     )

time: 120 us -> 81.8 us (0.68)
  local copies, waits for them, and re-layouts: 29.9 us -> 13.5 us
  matrix products: 20.4 us -> 6.33 us
  Pallas kernels: 60.8 us -> 57 us
  other arithmetic: 6.81 us -> 3.55 us
    pallas_call x4 -> x1, Pallas kernels: 48 us -> 11.4 us  [exchange(): pl.pallas_call(functools.partial(exchange_kernel, moves), out_shape=[jax....]
    pallas_call x0 -> x1, Pallas kernels: none -> 32.4 us  [align_update(): pl.pallas_call(functools.partial(align_kernel, seqs, part), out_shape=[ja...]
    dot_general x11 -> x1, matrix products: 12.1 us -> 0.35 us  [local(): jnp.einsum('ijc,ch->jhi', pair_normed, w_bias, preferred_element_type=jnp...]
    reshape x11 -> x1, local copies, waits for them, and re-layouts: 7.39 us -> 0.12 us  [local(): bias.reshape(tile_second, -1)]
    slice x8 -> x1, local copies, waits for them, and re-layouts: 2.78 us -> 0.01 us  [align_update(): w_right = spread_out(w_factor[:, FACTOR_CHANNELS:])]
    convert_element_type x8 -> x0, local copies, waits for them, and re-layouts: 2.4 us -> none  [the longest x1 0.97 us: column_attention(): row_entries.astype(jnp.float32) + project(gated_output, output_weight)]
    sub x2 -> x0, matrix products: 2.26 us -> none  [attend(): attention = jax.nn.softmax(scores, axis=-1).astype(jnp.bfloat16)]
    reduce_sum x5 -> x2, other arithmetic: 2.26 us -> 0.8 us  [layer_norm(): variance = jnp.mean(jnp.square(inputs - average), axis=-1, keepdims=True)]
where the time goes in v2:
time: 81.8 us; the launch traced here: 81.6 us
  Pallas kernels  57 us (70%)
  local copies, waits for them, and re-layouts  13.5 us (17%)
  matrix products  6.33 us (8%)
  other arithmetic  3.55 us (4%)
  between operations  1.15 us (1%)
    pallas_call x1, Pallas kernels, align_update(): pl.pallas_call(functools.partial(align_kernel, seqs, part), out_shape=[ja...  32.4 us
    pallas_call x1, Pallas kernels, mix_channels(): pl.pallas_call(mix_kernel, out_shape=out, in_specs=[vmem, vmem], out_spec...  13.2 us
    pallas_call x1, Pallas kernels, exchange(): pl.pallas_call(functools.partial(exchange_kernel, moves), out_shape=[jax....  11.4 us
    unnamed x41, local copies, waits for them, and re-layouts  3.83 us
    reshape x1, local copies, waits for them, and re-layouts, local(): left_slots.reshape(rows, branch_width, tile_first, tile_second)  2.8 us
    dot_general x1, matrix products, outer_mean(): jnp.einsum('sic,sje->ijce', left_factor, right_factor, preferred_element_...  2.32 us
    dot_general x1, matrix products, local(): jnp.einsum('rcik,rcjk->cij', left_slots.reshape(rows, branch_width, tile_...  1.89 us
    reshape x1, local copies, waits for them, and re-layouts, local(): right_slots.reshape(rows, branch_width, tile_second, tile_second)  1.73 us

profile of v2, /device:TPU:0, one launch (start us, length us, event | category | flops | bytes accessed | tf_op | source)
XLA Modules:
  0.0 81.6 jit_solution(5369324849626719981)
XLA Ops:
  0.7 1.8 %copy.61 = bf16[64,32,128]{0,2,1:T(8,128)(2,1)S(1)} copy(bf16[64,32,128]{2,1,0:T(8,128)(2,1)} %param.16) | data formatting | bytes 1048576 | tf_op args[1]
  2.5 0.2 convert_reduce_fusion
  2.8 0.4 fusion.4
  3.2 0.4 fusion.10
  3.6 0.1 reshape.103.bias_ref
  4.0 0.1 copy.63
  4.3 32.4 %shard_map.158 = (bf16[256,256]{1,0:T(8,128)(2,1)S(1)}, bf16[16,64,128]{2,1,0:T(8,128)(2,1)S(1)}, bf16[8,64,128]{2,1,0:T(8,128)(2,1)S(1)}) custom-call(bf16[256,256]{1,0:T(8,128)(2,1)S(1)} %bitcast.66, bf16[32,512]{1,0:T(8,128)(2,1)S(1)} %reshape.103.bias_ref, bf16[256,1024]{1,0:T(8,128)(2,1)S(1)} %copy-done.1, bf16[256,256]{1,0:T(8,128)(2,1)S(1)} %copy-done.4, ...), custom_call_target="tpu_custom_call" | custom-call | tf_op jit(solution)/shard_map/pallas_call | solution.py:579
  36.7 0.2 copy.65
  36.9 0.3 copy.66
  37.2 0.6 copy.67
  37.8 2.3 %multiply_convert_fusion = bf16[32,32,64,32]{2,1,3,0:T(8,128)(2,1)S(1)} fusion(bf16[64,32,32,1]{0,2,3,1:T(8,128)(2,1)S(1)} %bitcast.72, bf16[64,64,32]{1,0,2:T(8,128)(2,1)S(1)} %copy.67), kind=kOutput, calls=%fused_computation | convolution fusion | flops 272629760 | bytes 4587520 | tf_op jit(solution)/shard_map/sic,sje->ijce/dot_general | solution.py:85
  40.1 1.4 %convert_reduce_fusion.1 = (f32[64,32]{0,1:T(8,128)S(1)}, bf16[64,32,128]{0,2,1:T(8,128)(2,1)S(1)}) fusion(bf16[64,32,1024]{0,2,1:T(8,128)(2,1)S(1)} %bitcast.69, bf16[1024,128]{1,0:T(8,128)(2,1)S(1)} %copy-done, bf16[64,32,128]{0,2,1:T(8,128)(2,1)S(1)} %copy-done.10), kind=kOutput, calls=%fused_computation.5 | convolution fusion | flops 538703872 | bytes 5513216 | tf_op jit(solution)/shard_map/dot_general | solution.py:89
  41.7 0.4 copy.70
  42.1 0.5 reshape.114
  42.6 0.4 fusion.6
  43.0 0.4 fusion.7
  43.4 0.8 %copy.73 = bf16[64,32,128]{2,1,0:T(8,128)(2,1)S(1)} copy(bf16[64,32,128]{0,2,1:T(8,128)(2,1)S(1)} %fusion.7) | data formatting | bytes 1048576 | tf_op jit(solution)/shard_map/convert_element_type | solution.py:733
  44.4 0.1 copy.71
  44.6 0.3 fusion.31
  44.9 1.0 %fusion.15 = (bf16[32,2048]{1,0:T(8,128)(2,1)S(1)}, bf16[32,2048]{1,0:T(8,128)(2,1)}) fusion(f32[160,2048]{1,0:T(8,128)S(1)} %fusion.31), kind=kLoop, calls=%fused_computation.24 | loop fusion | flops 655360 | bytes 1310720 | tf_op jit(solution)/shard_map/convert_element_type | solution.py:745
  45.9 0.7 copy.90
  46.5 11.4 %shard_map.159 = (bf16[4,32,2048]{2,1,0:T(8,128)(2,1)}, bf16[4,32,1024]{2,1,0:T(8,128)(2,1)}) custom-call(bf16[32,2048]{1,0:T(8,128)(2,1)} %get-tuple-element.21.refs_0_, bf16[2,32,1024]{2,1,0:T(8,128)(2,1)} %bitcast.75), custom_call_target="tpu_custom_call" | custom-call | tf_op jit(solution)/shard_map/pallas_call | solution.py:367
  58.0 2.8 %reshape.110 = bf16[4,32,64,32]{3,2,1,0:T(8,128)(2,1)S(1)} reshape(bf16[4,32,2048]{2,1,0:T(8,128)(2,1)} %get-tuple-element.10) | data formatting | bytes 1048576 | tf_op jit(solution)/shard_map/reshape | solution.py:754
  60.8 1.7 %reshape.111 = bf16[4,32,32,32]{3,2,1,0:T(8,128)(2,1)} reshape(bf16[4,32,1024]{2,1,0:T(8,128)(2,1)S(1)} %copy-done.12) | data formatting | bytes 524288 | tf_op jit(solution)/shard_map/reshape | solution.py:755
  62.6 1.9 %fusion.9 = bf16[32,64,32]{1,2,0:T(8,128)(2,1)S(1)} fusion(bf16[4,32,64,32]{3,2,1,0:T(8,128)(2,1)S(1)} %reshape.110, bf16[4,32,32,32]{3,2,1,0:T(8,128)(2,1)} %reshape.111), kind=kOutput, calls=%fused_computation.17 | convolution fusion | flops 16842752 | bytes 917504 | tf_op jit(solution)/shard_map/rcik,rcjk->cij/dot_general | solution.py:752
  64.4 0.3 copy.76
  64.7 0.4 reshape.112
  65.2 13.2 %shard_map.160 = bf16[4,32,512]{2,1,0:T(8,128)(2,1)S(1)} custom-call(bf16[4,32,512]{2,1,0:T(8,128)(2,1)S(1)} %bitcast.64, bf16[128,128]{1,0:T(8,128)(2,1)S(1)} %copy-done.8), custom_call_target="tpu_custom_call" | custom-call | tf_op jit(solution)/shard_map/pallas_call | solution.py:402
  78.4 1.0 %fusion.30 = bf16[2048,32]{0,1:T(8,128)(2,1)S(1)} fusion(f32[2048,32]{0,1:T(8,128)S(1)} %reshape.114, f32[32,2048]{1,0:T(8,128)S(1)} %bitcast.73, f32[160,2048]{1,0:T(8,128)} %copy-done.11), kind=kLoop, calls=%fused_computation.45 | loop fusion | flops 393216 | bytes 917504 | tf_op jit(solution)/shard_map/convert_element_type | solution.py:763
  79.5 0.4 reshape.113
  79.8 1.1 %copy.79 = bf16[64,32,32]{0,2,1:T(8,128)(2,1)} copy(bf16[64,32,32]{1,0,2:T(8,128)(2,1)S(1)} %reshape.113) | data formatting | bytes 262144
  80.9 0.7 copy.93
  (54 shorter events, 0.7 us)
Async XLA Ops:
  0.6 39.5 %copy-start = (bf16[1024,128]{1,0:T(8,128)(2,1)S(1)}, bf16[1024,128]{1,0:T(8,128)(2,1)}, u32[]{:S(2)}) copy-start(bf16[1024,128]{1,0:T(8,128)(2,1)} %param.23) | copy-start | bytes 786436
  0.6 2.6 %copy-start.17 = (bf16[128,8]{0,1:T(8,128)(2,1)S(1)}, bf16[128,8]{0,1:T(8,128)(2,1)}, u32[]{:S(2)}) copy-start(bf16[128,8]{0,1:T(8,128)(2,1)} %param.19) | copy-start | bytes 6148
  2.4 1.3 %copy-start.9 = (bf16[64,32,128]{0,2,1:T(8,128)(2,1)}, bf16[64,32,128]{0,2,1:T(8,128)(2,1)S(1)}, u32[]{:S(2)}) copy-start(bf16[64,32,128]{0,2,1:T(8,128)(2,1)S(1)} %copy.61) | copy-start | bytes 1572868
  2.4 1.3 %copy-start.14 = (bf16[256,64]{0,1:T(8,128)(2,1)S(1)}, bf16[256,64]{0,1:T(8,128)(2,1)}, u32[]{:S(2)}) copy-start(bf16[256,64]{0,1:T(8,128)(2,1)} %param.22) | copy-start | bytes 98308
  2.4 1.4 %copy-start.16 = (bf16[4,4]{1,0:T(4,128)(2,1)S(1)}, bf16[4,4]{1,0:T(4,128)(2,1)}, u32[]{:S(2)}) copy-start(bf16[4,4]{1,0:T(4,128)(2,1)} %constant.33.clone) | copy-start | bytes 100
  2.7 1.5 %copy-start.1 = (bf16[256,1024]{1,0:T(8,128)(2,1)S(1)}, bf16[256,1024]{1,0:T(8,128)(2,1)}, u32[]{:S(2)}) copy-start(bf16[256,1024]{1,0:T(8,128)(2,1)} %w_row_ref.1) | copy-start | bytes 1572868
  2.7 1.5 %copy-start.2 = (bf16[256,1024]{1,0:T(8,128)(2,1)S(1)}, bf16[256,1024]{1,0:T(8,128)(2,1)}, u32[]{:S(2)}) copy-start(bf16[256,1024]{1,0:T(8,128)(2,1)} %w_col_ref.1) | copy-start | bytes 1572868
  2.7 1.5 %copy-start.3 = (bf16[4,64,256]{2,1,0:T(8,128)(2,1)S(1)}, bf16[4,64,256]{2,1,0:T(8,128)(2,1)}, u32[]{:S(2)}) copy-start(bf16[4,64,256]{2,1,0:T(8,128)(2,1)} %param.15) | copy-start | bytes 393220
  2.7 1.5 %copy-start.4 = (bf16[256,256]{1,0:T(8,128)(2,1)S(1)}, bf16[256,256]{1,0:T(8,128)(2,1)}, u32[]{:S(2)}) copy-start(bf16[256,256]{1,0:T(8,128)(2,1)} %row_out_ref.1) | copy-start | bytes 393220
  2.7 1.5 %copy-start.5 = (bf16[256,256]{1,0:T(8,128)(2,1)S(1)}, bf16[256,256]{1,0:T(8,128)(2,1)}, u32[]{:S(2)}) copy-start(bf16[256,256]{1,0:T(8,128)(2,1)} %col_out_ref.1) | copy-start | bytes 393220
  2.8 1.5 %copy-start.6 = (bf16[256,256]{1,0:T(8,128)(2,1)S(1)}, bf16[256,256]{1,0:T(8,128)(2,1)}, u32[]{:S(2)}) copy-start(bf16[256,256]{1,0:T(8,128)(2,1)} %constant.31.clone.permute_ref) | copy-start | bytes 393220
  2.8 1.5 %copy-start.7 = (bf16[256,256]{1,0:T(8,128)(2,1)S(1)}, bf16[256,256]{1,0:T(8,128)(2,1)}, u32[]{:S(2)}) copy-start(bf16[256,256]{1,0:T(8,128)(2,1)} %constant.32.clone.same_ref) | copy-start | bytes 393220
  37.8 2.3 %copy-start.10 = (bf16[64,32,128]{0,2,1:T(8,128)(2,1)S(1)}, bf16[64,32,128]{0,2,1:T(8,128)(2,1)}, u32[]{:S(2)}) copy-start(bf16[64,32,128]{0,2,1:T(8,128)(2,1)} %copy-done.9) | copy-start | bytes 1572868
  43.0 1.3 %copy-start.15 = (bf16[128,128]{1,0:T(8,128)(2,1)S(1)}, bf16[128,128]{1,0:T(8,128)(2,1)}, u32[]{:S(2)}) copy-start(bf16[128,128]{1,0:T(8,128)(2,1)} %param.25) | copy-start | bytes 98308
  43.0 1.4 %copy-start.13 = (bf16[128,512]{1,0:T(8,128)(2,1)S(1)}, bf16[128,512]{1,0:T(8,128)(2,1)}, u32[]{:S(2)}) copy-start(bf16[128,512]{1,0:T(8,128)(2,1)} %param.24) | copy-start | bytes 393220
  44.9 13.1 %copy-start.11 = (f32[160,2048]{1,0:T(8,128)}, f32[160,2048]{1,0:T(8,128)S(1)}, u32[]{:S(2)}) copy-start(f32[160,2048]{1,0:T(8,128)S(1)} %fusion.31) | copy-start | bytes 3932164
  58.0 2.8 %copy-start.12 = (bf16[4,32,1024]{2,1,0:T(8,128)(2,1)S(1)}, bf16[4,32,1024]{2,1,0:T(8,128)(2,1)}, u32[]{:S(2)}) copy-start(bf16[4,32,1024]{2,1,0:T(8,128)(2,1)} %get-tuple-element.11) | copy-start | bytes 786436
  62.6 2.6 %copy-start.8 = (bf16[128,128]{1,0:T(8,128)(2,1)S(1)}, bf16[128,128]{1,0:T(8,128)(2,1)}, u32[]{:S(2)}) copy-start(bf16[128,128]{1,0:T(8,128)(2,1)} %weight_ref.1) | copy-start | bytes 98308

commit v3 on v2

--- a/solution.py
+++ b/solution.py
@@ -604,6 +604,50 @@
     return out.reshape(alignment.shape), left_slots, right_slots
 
 
+def triangle_kernel(width, left_ref, right_ref, out_ref, left_slots, right_slots, *sems):
+    over_row, aim = Regular(("row",), False), ColToRow(False)
+    total = over_row.greet() + aim.greet()
+    pl.semaphore_wait(pltpu.get_barrier_semaphore(), total)
+    over_row.start(left_ref, left_slots, sems[0:2])
+    aim.start(right_ref, right_slots, sems[2:5])
+    over_row.wait(left_ref, left_slots, sems[0:2])
+    aim.wait(right_ref, right_slots, sems[2:5])
+    left = left_slots[...].reshape(-1, left_ref.shape[-1])
+    right = right_slots[...].reshape(-1, right_ref.shape[-1])
+    first, second = left.shape[1] // width, right.shape[1] // width
+    batch = max(1, 128 // min(first, second))
+    for start in range(0, width, batch):
+        product = dot(
+            left[:, start * first : (start + batch) * first],
+            right[:, start * second : (start + batch) * second],
+            0,
+            0,
+        )
+        for c in range(batch):
+            out_ref[start + c] = product[
+                c * first : (c + 1) * first, c * second : (c + 1) * second
+            ].astype(out_ref.dtype)
+
+
+def triangle_product(collective_id, left, right, width):
+    over_row, aim = Regular(("row",), False), ColToRow(False)
+    vmem = pl.BlockSpec(memory_space=pltpu.VMEM)
+    slots = [over_row.slots(left), aim.slots(right)]
+    shape = (width, left.shape[1] // width, right.shape[2] // width)
+    return pl.pallas_call(
+        functools.partial(triangle_kernel, width),
+        out_shape=jax.ShapeDtypeStruct(shape, jnp.bfloat16),
+        in_specs=[vmem] * 2,
+        out_specs=vmem,
+        scratch_shapes=[pltpu.VMEM(x.shape, x.dtype) for x in slots]
+        + over_row.semaphores()
+        + aim.semaphores(),
+        compiler_params=pltpu.CompilerParams(
+            collective_id=collective_id, has_side_effects=True, vmem_limit_bytes=48 << 20
+        ),
+    )(left, right)
+
+
 def align_unfused(
     alignment, pair_normed, w_row, row_output_weight, w_bias, w_column, column_output_weight,
     outer_input_weight,
@@ -736,25 +780,26 @@
         w_triangle_in.reshape(PAIR_WIDTH, 4, TRIANGLE_WIDTH), branch_start, branch_width, 2
     )
     gate_weight = lax.dynamic_slice_in_dim(w_triangle_gate, out_start, out_width, 1)
-    w_all = jnp.concatenate([w_in.reshape(PAIR_WIDTH, 4 * branch_width), gate_weight], axis=1)
-    projected = lax.dot_general(
-        w_all, flat_normed, (((0,), (1,)), ((), ())), preferred_element_type=jnp.float32
-    )
-    tri = projected[: 4 * branch_width].reshape(4, branch_width, -1)
+    tri = jnp.einsum(
+        "ikf,fpc->pkci", triangle_normed, w_in, preferred_element_type=jnp.float32
+    )
     tri_left = (jax.nn.sigmoid(tri[1]) * tri[0]).astype(jnp.bfloat16)
     tri_right = (jax.nn.sigmoid(tri[3]) * tri[2]).astype(jnp.bfloat16)
-    output_gate = jax.nn.sigmoid(projected[4 * branch_width :])
+    output_gate = jax.nn.sigmoid(
+        lax.dot_general(
+            gate_weight, flat_normed, (((0,), (1,)), ((), ())), preferred_element_type=jnp.float32
+        )
+    )
     per = rows // lax.axis_size("col")
-    right_parts = jnp.transpose(tri_right.reshape(branch_width, per, -1), (1, 0, 2))
-    left_slots, right_slots = exchange(
-        3, [Regular(("row",), False), ColToRow(False)], [tri_left, right_parts]
-    )
-    product = jnp.einsum(
-        "rcik,rcjk->cij",
-        left_slots.reshape(rows, branch_width, tile_first, tile_second),
-        right_slots.reshape(rows, branch_width, tile_second, tile_second),
-        preferred_element_type=jnp.float32,
-    ).astype(jnp.bfloat16)
+    right_parts = jnp.transpose(
+        tri_right.reshape(tile_second, branch_width, per, tile_second), (2, 0, 1, 3)
+    )
+    product = triangle_product(
+        3,
+        tri_left.reshape(tile_second, -1),
+        right_parts.reshape(per, tile_second, -1),
+        branch_width,
+    )
     sums = jnp.transpose(product.reshape(branch_width, groups, -1), (1, 0, 2))
     mixed = mix_channels(4, sums, w_triangle_out)
     mixed = jnp.transpose(mixed, (1, 0, 2)).reshape(out_width, -1)

time: 81.8 us -> 85.2 us (1.042)
  other arithmetic: 3.55 us -> 5.26 us
  matrix products: 6.33 us -> 7.71 us
    unnamed x41 -> x27, local copies, waits for them, and re-layouts: 3.83 us -> 8.5 us
    reshape x2 -> x1, local copies, waits for them, and re-layouts: 4.54 us -> 0.53 us  [local(): right_parts.reshape(per, tile_second, -1)]
    reduce_sum x1 -> x2, other arithmetic: 0.23 us -> 1.87 us  [layer_norm(): average = jnp.mean(inputs, axis=-1, keepdims=True)]
    dot_general x1, matrix products: 0.35 us -> 1.9 us  [local(): jnp.einsum('ijc,ch->jhi', pair_normed, w_bias, preferred_element_type=jnp...]
    reduce_sum x2, other arithmetic: 0.8 us -> 2.3 us  [layer_norm(): variance = jnp.mean(jnp.square(inputs - average), axis=-1, keepdims=True)]
    dot_general x2, matrix products: 2.21 us -> 1.09 us  [the longest x1 0.69 us: local(): jnp.einsum('ikf,fpc->pkci', triangle_normed, w_in, preferred_element_type...]
    convert_element_type x2 -> x1, other arithmetic: 1.09 us -> 0.1 us  [local(): pair_out = (pair_slice.astype(jnp.float32) + update).astype(jnp.bfloat16)]
    dot_general x1, matrix products: 1.44 us -> 2.4 us  [outer_mean(): jnp.dot(flat_rows, w_outer_out, preferred_element_type=jnp.float32)]
where the time goes in v3:
time: 85.2 us; the launch traced here: 84.8 us
  Pallas kernels  56.7 us (67%)
  local copies, waits for them, and re-layouts  14.1 us (17%)
  matrix products  7.71 us (9%)
  other arithmetic  5.26 us (6%)
  between operations  0.97 us (1%)
    pallas_call x1, Pallas kernels, align_update(): pl.pallas_call(functools.partial(align_kernel, seqs, part), out_shape=[ja...  32.1 us
    pallas_call x1, Pallas kernels, mix_channels(): pl.pallas_call(mix_kernel, out_shape=out, in_specs=[vmem, vmem], out_spec...  12.9 us
    pallas_call x1, Pallas kernels, triangle_product(): pl.pallas_call(functools.partial(triangle_kernel, width), out_shape=jax.S...  11.7 us
    unnamed x27, local copies, waits for them, and re-layouts  8.5 us
    dot_general x1, matrix products, outer_mean(): jnp.dot(flat_rows, w_outer_out, preferred_element_type=jnp.float32)  2.4 us
    dot_general x1, matrix products, outer_mean(): jnp.einsum('sic,sje->ijce', left_factor, right_factor, preferred_element_...  2.32 us
    reduce_sum x2, other arithmetic, layer_norm(): variance = jnp.mean(jnp.square(inputs - average), axis=-1, keepdims=True)  2.3 us
    dot_general x1, matrix products, local(): jnp.einsum('ijc,ch->jhi', pair_normed, w_bias, preferred_element_type=jnp...  1.9 us

profile of v3, /device:TPU:0, one launch (start us, length us, event | category | flops | bytes accessed | tf_op | source)
XLA Modules:
  0.0 84.8 jit_solution(6535592270932241578)
XLA Ops:
  0.6 1.4 %convert_reduce_fusion = f32[64,32]{1,0:T(8,128)S(1)} fusion(bf16[64,32,128]{2,1,0:T(8,128)(2,1)} %param.16), kind=kLoop, calls=%fused_computation.12 | loop fusion | flops 522240 | bytes 532480 | tf_op jit(solution)/shard_map/reduce_sum | solution.py:24
  2.1 1.7 %fusion.12 = f32[64,32]{1,0:T(8,128)S(1)} fusion(bf16[64,32,128]{2,1,0:T(8,128)(2,1)} %param.16, f32[64,32]{1,0:T(8,128)S(1)} %broadcast_multiply_fusion.3), kind=kLoop, calls=%fused_computation.21 | loop fusion | flops 1046528 | bytes 540672 | tf_op jit(solution)/shard_map/reduce_sum | solution.py:25
  3.8 1.9 %fusion.11 = bf16[32,8,64]{0,1,2:T(8,128)(2,1)S(1)} fusion(bf16[64,32,128]{2,1,0:T(8,128)(2,1)} %param.16, f32[64,32]{1,0:T(8,128)S(1)} %add_rsqrt_fusion.1, f32[64,32]{1,0:T(8,128)S(1)} %broadcast_multiply_fusion.3, bf16[128,8]{0,1:T(8,128)(2,1)} %param.19), kind=kOutput, calls=%fused_computation.20 | convolution fusion | flops 5259264 | bytes 575488 | tf_op jit(solution)/shard_map/ijc,ch->jhi/dot_general | solution.py:737
  6.0 0.7 fusion.40
  6.8 0.8 mul.78
  7.9 1.0 %copy-done.1 = bf16[256,1024]{1,0:T(8,128)(2,1)S(1)} copy-done((bf16[256,1024]{1,0:T(8,128)(2,1)S(1)}, bf16[256,1024]{1,0:T(8,128)(2,1)}, u32[]{:S(2)}) %copy-start.1) | copy-done | bytes 524312
  8.9 1.0 %copy-done.2 = bf16[256,1024]{1,0:T(8,128)(2,1)S(1)} copy-done((bf16[256,1024]{1,0:T(8,128)(2,1)S(1)}, bf16[256,1024]{1,0:T(8,128)(2,1)}, u32[]{:S(2)}) %copy-start.2) | copy-done | bytes 524312
  9.9 0.9 %copy-done.3 = bf16[4,64,256]{2,1,0:T(8,128)(2,1)S(1)} copy-done((bf16[4,64,256]{2,1,0:T(8,128)(2,1)S(1)}, bf16[4,64,256]{2,1,0:T(8,128)(2,1)}, u32[]{:S(2)}) %copy-start.3) | copy-done | bytes 131096
  10.9 0.9 %copy-done.4 = bf16[256,256]{1,0:T(8,128)(2,1)S(1)} copy-done((bf16[256,256]{1,0:T(8,128)(2,1)S(1)}, bf16[256,256]{1,0:T(8,128)(2,1)}, u32[]{:S(2)}) %copy-start.4) | copy-done | bytes 131096
  11.8 0.9 %copy-done.5 = bf16[256,256]{1,0:T(8,128)(2,1)S(1)} copy-done((bf16[256,256]{1,0:T(8,128)(2,1)S(1)}, bf16[256,256]{1,0:T(8,128)(2,1)}, u32[]{:S(2)}) %copy-start.5) | copy-done | bytes 131096
  12.7 0.9 %copy-done.6 = bf16[256,256]{1,0:T(8,128)(2,1)S(1)} copy-done((bf16[256,256]{1,0:T(8,128)(2,1)S(1)}, bf16[256,256]{1,0:T(8,128)(2,1)}, u32[]{:S(2)}) %copy-start.6) | copy-done | bytes 131096
  13.6 0.9 %copy-done.7 = bf16[256,256]{1,0:T(8,128)(2,1)S(1)} copy-done((bf16[256,256]{1,0:T(8,128)(2,1)S(1)}, bf16[256,256]{1,0:T(8,128)(2,1)}, u32[]{:S(2)}) %copy-start.7) | copy-done | bytes 131096
  14.5 32.1 %shard_map.158 = (bf16[256,256]{1,0:T(8,128)(2,1)S(1)}, bf16[16,64,128]{2,1,0:T(8,128)(2,1)S(1)}, bf16[8,64,128]{2,1,0:T(8,128)(2,1)S(1)}) custom-call(bf16[256,256]{1,0:T(8,128)(2,1)S(1)} %bitcast.70, bf16[32,512]{1,0:T(8,128)(2,1)S(1)} %reshape.97.bias_ref, bf16[256,1024]{1,0:T(8,128)(2,1)S(1)} %copy-done.1, bf16[256,256]{1,0:T(8,128)(2,1)S(1)} %copy-done.4, ...), custom_call_target="tpu_custom_call" | custom-call | tf_op jit(solution)/shard_map/pallas_call | solution.py:579
  46.8 0.3 copy.30
  47.1 0.6 copy.31
  47.7 2.3 %multiply_convert_fusion = bf16[32,32,64,32]{2,1,3,0:T(8,128)(2,1)S(1)} fusion(bf16[64,32,32,1]{0,2,3,1:T(8,128)(2,1)S(1)} %bitcast.77, bf16[64,64,32]{1,0,2:T(8,128)(2,1)S(1)} %copy.31), kind=kOutput, calls=%fused_computation | convolution fusion | flops 272629760 | bytes 4587520 | tf_op jit(solution)/shard_map/sic,sje->ijce/dot_general | solution.py:85
  50.1 2.4 %fusion.31 = bf16[64,32,128]{2,0,1:T(8,128)(2,1)S(1)} fusion(bf16[64,32,1024]{0,2,1:T(8,128)(2,1)S(1)} %bitcast.73, bf16[1024,128]{1,0:T(8,128)(2,1)S(1)} %copy-done), kind=kOutput, calls=%fused_computation.46 | convolution fusion | flops 536870912 | bytes 4980736 | tf_op jit(solution)/shard_map/dot_general | solution.py:89
  52.5 0.4 convert_reduce_fusion.1
  53.3 0.3 copy.38
  53.6 0.6 fusion.14
  54.3 0.6 fusion.15
  55.0 0.7 convolution_bitcast_fusion
  55.7 0.3 fusion.18
  56.0 0.3 reshape.110.left_ref
  56.6 0.5 reshape.103.right_ref
  57.1 11.7 %shard_map.159 = bf16[32,64,32]{2,1,0:T(8,128)(2,1)S(1)} custom-call(bf16[32,2048]{1,0:T(8,128)(2,1)S(1)} %reshape.110.left_ref, bf16[2,32,1024]{2,1,0:T(8,128)(2,1)S(1)} %reshape.103.right_ref), custom_call_target="tpu_custom_call" | custom-call | tf_op jit(solution)/shard_map/pallas_call | solution.py:637
  68.8 0.4 reshape.104
  69.3 12.9 %shard_map.160 = bf16[4,32,512]{2,1,0:T(8,128)(2,1)S(1)} custom-call(bf16[4,32,512]{2,1,0:T(8,128)(2,1)S(1)} %bitcast.68, bf16[128,128]{1,0:T(8,128)(2,1)S(1)} %copy-done.8), custom_call_target="tpu_custom_call" | custom-call | tf_op jit(solution)/shard_map/pallas_call | solution.py:402
  82.2 0.4 fusion.6
  82.6 0.4 reshape.105
  83.0 1.1 %copy.39 = bf16[64,32,32]{0,2,1:T(8,128)(2,1)} copy(bf16[64,32,32]{1,0,2:T(8,128)(2,1)S(1)} %reshape.105) | data formatting | bytes 262144
  84.1 0.7 copy.58
  (38 shorter events, 1.7 us)
Async XLA Ops:
  0.6 49.4 %copy-start = (bf16[1024,128]{1,0:T(8,128)(2,1)S(1)}, bf16[1024,128]{1,0:T(8,128)(2,1)}, u32[]{:S(2)}) copy-start(bf16[1024,128]{1,0:T(8,128)(2,1)} %param.23) | copy-start | bytes 786436
  7.9 1.0 %copy-start.1 = (bf16[256,1024]{1,0:T(8,128)(2,1)S(1)}, bf16[256,1024]{1,0:T(8,128)(2,1)}, u32[]{:S(2)}) copy-start(bf16[256,1024]{1,0:T(8,128)(2,1)} %w_row_ref.1) | copy-start | bytes 1572868
  8.9 1.0 %copy-start.2 = (bf16[256,1024]{1,0:T(8,128)(2,1)S(1)}, bf16[256,1024]{1,0:T(8,128)(2,1)}, u32[]{:S(2)}) copy-start(bf16[256,1024]{1,0:T(8,128)(2,1)} %w_col_ref.1) | copy-start | bytes 1572868
  9.9 0.9 %copy-start.3 = (bf16[4,64,256]{2,1,0:T(8,128)(2,1)S(1)}, bf16[4,64,256]{2,1,0:T(8,128)(2,1)}, u32[]{:S(2)}) copy-start(bf16[4,64,256]{2,1,0:T(8,128)(2,1)} %param.15) | copy-start | bytes 393220
  10.9 0.9 %copy-start.4 = (bf16[256,256]{1,0:T(8,128)(2,1)S(1)}, bf16[256,256]{1,0:T(8,128)(2,1)}, u32[]{:S(2)}) copy-start(bf16[256,256]{1,0:T(8,128)(2,1)} %row_out_ref.1) | copy-start | bytes 393220
  11.8 0.9 %copy-start.5 = (bf16[256,256]{1,0:T(8,128)(2,1)S(1)}, bf16[256,256]{1,0:T(8,128)(2,1)}, u32[]{:S(2)}) copy-start(bf16[256,256]{1,0:T(8,128)(2,1)} %col_out_ref.1) | copy-start | bytes 393220
  12.7 0.9 %copy-start.6 = (bf16[256,256]{1,0:T(8,128)(2,1)S(1)}, bf16[256,256]{1,0:T(8,128)(2,1)}, u32[]{:S(2)}) copy-start(bf16[256,256]{1,0:T(8,128)(2,1)} %constant.32.clone.permute_ref) | copy-start | bytes 393220
  13.6 0.9 %copy-start.7 = (bf16[256,256]{1,0:T(8,128)(2,1)S(1)}, bf16[256,256]{1,0:T(8,128)(2,1)}, u32[]{:S(2)}) copy-start(bf16[256,256]{1,0:T(8,128)(2,1)} %constant.33.clone.same_ref) | copy-start | bytes 393220
  50.0 2.4 %copy-start.9 = (bf16[64,32,128]{2,1,0:T(8,128)(2,1)S(1)}, bf16[64,32,128]{2,1,0:T(8,128)(2,1)}, u32[]{:S(2)}) copy-start(bf16[64,32,128]{2,1,0:T(8,128)(2,1)} %param.16) | copy-start | bytes 1572868
  50.0 4.8 %copy-start.10 = (bf16[128,512]{1,0:T(8,128)(2,1)S(1)}, bf16[128,512]{1,0:T(8,128)(2,1)}, u32[]{:S(2)}) copy-start(bf16[128,512]{1,0:T(8,128)(2,1)} %param.24) | copy-start | bytes 393220
  52.5 16.8 %copy-start.8 = (bf16[128,128]{1,0:T(8,128)(2,1)S(1)}, bf16[128,128]{1,0:T(8,128)(2,1)}, u32[]{:S(2)}) copy-start(bf16[128,128]{1,0:T(8,128)(2,1)} %weight_ref.1) | copy-start | bytes 98308
  52.9 29.3 %copy-start.11 = (bf16[128,128]{1,0:T(8,128)(2,1)S(1)}, bf16[128,128]{1,0:T(8,128)(2,1)}, u32[]{:S(2)}) copy-start(bf16[128,128]{1,0:T(8,128)(2,1)} %param.25) | copy-start | bytes 98308

commit v4 on v3

--- a/solution.py
+++ b/solution.py
@@ -433,14 +433,14 @@
     part,
     align_ref,
     bias_ref,
-    w_row_ref,
-    row_out_ref,
-    w_col_ref,
-    col_out_ref,
-    w_left_ref,
-    w_right_ref,
-    permute_ref,
-    same_ref,
+    w_row_far,
+    row_out_far,
+    w_col_far,
+    col_out_far,
+    w_left_far,
+    w_right_far,
+    permute_far,
+    same_far,
     out_ref,
     left_slots,
     right_slots,
@@ -454,8 +454,34 @@
     normed_cols,
     left,
     right,
+    w_row_ref,
+    row_out_ref,
+    w_col_ref,
+    col_out_ref,
+    w_left_ref,
+    w_right_ref,
+    permute_ref,
+    same_ref,
+    weight_sems,
     *sems,
 ):
+    fetches = [
+        pltpu.make_async_copy(far, near, weight_sems.at[n])
+        for n, (far, near) in enumerate(
+            (
+                (w_row_far, w_row_ref),
+                (row_out_far, row_out_ref),
+                (permute_far, permute_ref),
+                (w_col_far, w_col_ref),
+                (col_out_far, col_out_ref),
+                (w_left_far, w_left_ref),
+                (w_right_far, w_right_ref),
+                (same_far, same_ref),
+            )
+        )
+    ]
+    for fetch in fetches:
+        fetch.start()
     bf16, width = jnp.bfloat16, ALIGN_CHANNELS
     group_axes = ("branch", "row")
     groups = group_size(group_axes)
@@ -467,6 +493,7 @@
     normed[...] = layer_norm(align_ref[...]).astype(bf16)
     over_col.start(normed, gathered, sems[2:4])
     residues = align_ref.shape[0] // seqs
+    fetches[0].wait()
     lanes = lax.broadcasted_iota(jnp.int32, (residues, width), 1)
     picks = [
         (lanes >= h * HEAD_CHANNELS) & (lanes < (h + 1) * HEAD_CHANNELS) for h in range(HEAD_COUNT)
@@ -493,9 +520,13 @@
             attended = jnp.where(p, spreadout[h * residues : (h + 1) * residues], attended)
         mixed.append(attended)
     row_gated = (gate * jnp.concatenate(mixed, axis=0)).astype(bf16)
+    fetches[1].wait()
+    fetches[2].wait()
     updated = align_ref[...].astype(jnp.float32) + dot(row_gated, row_out_ref[...])
     outgoing[...] = dot(permute_ref[...], updated.astype(bf16)).astype(bf16).reshape(outgoing.shape)
     swap.start(outgoing, columns, sems[4:6])
+    for fetch in fetches[3:]:
+        fetch.wait()
     swap.wait(outgoing, columns, sems[4:6])
     entries = columns[...].reshape(-1, width)
     count = entries.shape[0]
@@ -572,10 +603,14 @@
         pltpu.VMEM(factor.shape, bf16),
         pltpu.VMEM(factor.shape, bf16),
     ]
+    weights = (w_row, row_out, w_col, col_out, w_left, w_right, permute, same)
+    scratch += [pltpu.VMEM(w.shape, w.dtype) for w in weights]
+    scratch += [pltpu.SemaphoreType.DMA((len(weights),))]
     for move in (over_row, over_col, swap, swap, spread, aim):
         scratch += move.semaphores()
     vmem = pl.BlockSpec(memory_space=pltpu.VMEM)
     anywhere = pl.BlockSpec(memory_space=pl.ANY)
+    far = pl.BlockSpec(memory_space=pltpu.MemorySpace.HBM)
     out, left_slots, right_slots = pl.pallas_call(
         functools.partial(align_kernel, seqs, part),
         out_shape=[
@@ -583,23 +618,16 @@
             spread.slots(factor),
             aim.slots(factor),
         ],
-        in_specs=[vmem] * 10,
+        in_specs=[vmem] * 2 + [far] * 8,
         out_specs=[vmem, anywhere, anywhere],
         scratch_shapes=scratch,
         compiler_params=pltpu.CompilerParams(
-            collective_id=collective_id, has_side_effects=True, vmem_limit_bytes=48 << 20
+            collective_id=collective_id, has_side_effects=True, vmem_limit_bytes=60 << 20
         ),
     )(
         alignment.reshape(count, width),
         bias,
-        w_row,
-        row_out,
-        w_col,
-        col_out,
-        w_left,
-        w_right,
-        permute,
-        same,
+        *weights,
     )
     return out.reshape(alignment.shape), left_slots, right_slots
 

time: 85.2 us -> 83.8 us (0.984)
  local copies, waits for them, and re-layouts: 14.1 us -> 9.97 us
  Pallas kernels: 56.7 us -> 58.8 us
    unnamed x27 -> x15, local copies, waits for them, and re-layouts: 8.5 us -> 1.91 us
    pallas_call x1, Pallas kernels: 32.1 us -> 34 us  [align_update(): pl.pallas_call(functools.partial(align_kernel, seqs, part), out_shape=[ja...]
    transpose x1, local copies, waits for them, and re-layouts: 0.29 us -> 1.23 us  [local(): jnp.transpose(left_slots, (1, 0, 2))]
    transpose x1, local copies, waits for them, and re-layouts: 0.18 us -> 1.07 us  [local(): jnp.transpose(right_slots, (1, 0, 2))]
where the time goes in v4:
time: 83.8 us; the launch traced here: 83.5 us
  Pallas kernels  58.8 us (70%)
  local copies, waits for them, and re-layouts  9.97 us (12%)
  matrix products  7.72 us (9%)
  other arithmetic  6.04 us (7%)
  between operations  0.96 us (1%)
    pallas_call x1, Pallas kernels, align_update(): pl.pallas_call(functools.partial(align_kernel, seqs, part), out_shape=[ja...  34 us
    pallas_call x1, Pallas kernels, mix_channels(): pl.pallas_call(mix_kernel, out_shape=out, in_specs=[vmem, vmem], out_spec...  13.1 us
    pallas_call x1, Pallas kernels, triangle_product(): pl.pallas_call(functools.partial(triangle_kernel, width), out_shape=jax.S...  11.7 us
    dot_general x1, matrix products, outer_mean(): jnp.dot(flat_rows, w_outer_out, preferred_element_type=jnp.float32)  2.4 us
    dot_general x1, matrix products, outer_mean(): jnp.einsum('sic,sje->ijce', left_factor, right_factor, preferred_element_...  2.32 us
    reduce_sum x2, other arithmetic, layer_norm(): variance = jnp.mean(jnp.square(inputs - average), axis=-1, keepdims=True)  2.3 us
    unnamed x15, local copies, waits for them, and re-layouts  1.91 us
    dot_general x1, matrix products, local(): jnp.einsum('ijc,ch->jhi', pair_normed, w_bias, preferred_element_type=jnp...  1.9 us

profile of v4, /device:TPU:0, one launch (start us, length us, event | category | flops | bytes accessed | tf_op | source)
XLA Modules:
  0.0 83.5 jit_solution(17676611781532203705)
XLA Ops:
  0.6 1.4 %convert_reduce_fusion = f32[64,32]{1,0:T(8,128)S(1)} fusion(bf16[64,32,128]{2,1,0:T(8,128)(2,1)} %param.16), kind=kLoop, calls=%fused_computation.12 | loop fusion | flops 522240 | bytes 532480 | tf_op jit(solution)/shard_map/reduce_sum | solution.py:24
  2.1 1.7 %fusion.12 = f32[64,32]{1,0:T(8,128)S(1)} fusion(bf16[64,32,128]{2,1,0:T(8,128)(2,1)} %param.16, f32[64,32]{1,0:T(8,128)S(1)} %broadcast_multiply_fusion.3), kind=kLoop, calls=%fused_computation.21 | loop fusion | flops 1046528 | bytes 540672 | tf_op jit(solution)/shard_map/reduce_sum | solution.py:25
  3.8 1.9 %fusion.11 = bf16[32,8,64]{0,1,2:T(8,128)(2,1)S(1)} fusion(bf16[64,32,128]{2,1,0:T(8,128)(2,1)} %param.16, f32[64,32]{1,0:T(8,128)S(1)} %add_rsqrt_fusion.1, f32[64,32]{1,0:T(8,128)S(1)} %broadcast_multiply_fusion.3, bf16[128,8]{0,1:T(8,128)(2,1)} %param.19), kind=kOutput, calls=%fused_computation.20 | convolution fusion | flops 5259264 | bytes 575488 | tf_op jit(solution)/shard_map/ijc,ch->jhi/dot_general | solution.py:765
  5.7 0.2 copy.26
  5.9 0.7 reshape.97.bias_ref
  6.6 0.7 fusion.40
  7.5 0.8 mul.78
  8.4 0.8 broadcast_multiply_fusion
  9.2 34.0 %shard_map.158 = (bf16[256,256]{1,0:T(8,128)(2,1)}, bf16[16,64,128]{2,1,0:T(8,128)(2,1)}, bf16[8,64,128]{2,1,0:T(8,128)(2,1)}) custom-call(bf16[256,256]{1,0:T(8,128)(2,1)} %bitcast.79, bf16[32,512]{1,0:T(8,128)(2,1)} %reshape.97.bias_ref, bf16[256,1024]{1,0:T(8,128)(2,1)} %w_row_far.1, bf16[256,256]{1,0:T(8,128)(2,1)} %row_out_far.1, ...), custom_call_target="tpu_custom_call" | custom-call | tf_op jit(solution)/shard_map/pallas_call | solution.py:614
  43.3 1.1 %copy.29 = bf16[64,8,128]{0,2,1:T(8,128)(2,1)S(1)} copy(bf16[64,8,128]{2,0,1:T(8,128)(2,1)} %bitcast.80) | data formatting | bytes 262144 | tf_op jit(solution)/shard_map/transpose | solution.py:793
  44.4 1.2 %copy.30 = bf16[64,16,128]{0,2,1:T(8,128)(2,1)S(1)} copy(bf16[64,16,128]{2,0,1:T(8,128)(2,1)} %bitcast.74) | data formatting | bytes 524288 | tf_op jit(solution)/shard_map/transpose | solution.py:790
  45.6 0.6 copy.31
  46.2 2.3 %multiply_convert_fusion = bf16[32,32,64,32]{2,1,3,0:T(8,128)(2,1)S(1)} fusion(bf16[64,32,32,1]{0,2,3,1:T(8,128)(2,1)S(1)} %bitcast.73, bf16[64,64,32]{1,0,2:T(8,128)(2,1)S(1)} %copy.31), kind=kOutput, calls=%fused_computation | convolution fusion | flops 272629760 | bytes 4587520 | tf_op jit(solution)/shard_map/sic,sje->ijce/dot_general | solution.py:85
  48.6 2.4 %fusion.31 = bf16[64,32,128]{2,0,1:T(8,128)(2,1)S(1)} fusion(bf16[64,32,1024]{0,2,1:T(8,128)(2,1)S(1)} %bitcast.69, bf16[1024,128]{1,0:T(8,128)(2,1)S(1)} %copy-done), kind=kOutput, calls=%fused_computation.46 | convolution fusion | flops 536870912 | bytes 4980736 | tf_op jit(solution)/shard_map/dot_general | solution.py:89
  51.0 0.4 convert_reduce_fusion.1
  51.5 0.2 constant_dynamic-slice_fusion
  51.8 0.3 copy.38
  52.1 0.6 fusion.14
  52.8 0.6 fusion.15
  53.4 0.1 copy.33
  53.5 0.7 convolution_bitcast_fusion
  54.2 0.3 fusion.18
  54.5 0.3 reshape.110.left_ref
  54.8 0.2 reshape.111
  55.1 0.5 reshape.103.right_ref
  55.7 11.7 %shard_map.159 = bf16[32,64,32]{2,1,0:T(8,128)(2,1)S(1)} custom-call(bf16[32,2048]{1,0:T(8,128)(2,1)S(1)} %reshape.110.left_ref, bf16[2,32,1024]{2,1,0:T(8,128)(2,1)S(1)} %reshape.103.right_ref), custom_call_target="tpu_custom_call" | custom-call | tf_op jit(solution)/shard_map/pallas_call | solution.py:665
  67.3 0.4 reshape.104
  67.8 13.1 %shard_map.160 = bf16[4,32,512]{2,1,0:T(8,128)(2,1)S(1)} custom-call(bf16[4,32,512]{2,1,0:T(8,128)(2,1)S(1)} %bitcast.68, bf16[128,128]{1,0:T(8,128)(2,1)S(1)} %copy-done.1), custom_call_target="tpu_custom_call" | custom-call | tf_op jit(solution)/shard_map/pallas_call | solution.py:402
  80.9 0.4 fusion.6
  81.3 0.4 reshape.105
  81.7 1.1 %copy.39 = bf16[64,32,32]{0,2,1:T(8,128)(2,1)} copy(bf16[64,32,32]{1,0,2:T(8,128)(2,1)S(1)} %reshape.105) | data formatting | bytes 262144
  82.8 0.7 copy.58
  (26 shorter events, 0.7 us)
Async XLA Ops:
  0.6 47.9 %copy-start = (bf16[1024,128]{1,0:T(8,128)(2,1)S(1)}, bf16[1024,128]{1,0:T(8,128)(2,1)}, u32[]{:S(2)}) copy-start(bf16[1024,128]{1,0:T(8,128)(2,1)} %param.23) | copy-start | bytes 786436
  48.5 2.4 %copy-start.2 = (bf16[64,32,128]{2,1,0:T(8,128)(2,1)S(1)}, bf16[64,32,128]{2,1,0:T(8,128)(2,1)}, u32[]{:S(2)}) copy-start(bf16[64,32,128]{2,1,0:T(8,128)(2,1)} %param.16) | copy-start | bytes 1572868
  48.6 4.8 %copy-start.3 = (bf16[128,512]{1,0:T(8,128)(2,1)S(1)}, bf16[128,512]{1,0:T(8,128)(2,1)}, u32[]{:S(2)}) copy-start(bf16[128,512]{1,0:T(8,128)(2,1)} %param.24) | copy-start | bytes 393220
  51.0 16.8 %copy-start.1 = (bf16[128,128]{1,0:T(8,128)(2,1)S(1)}, bf16[128,128]{1,0:T(8,128)(2,1)}, u32[]{:S(2)}) copy-start(bf16[128,128]{1,0:T(8,128)(2,1)} %weight_ref.1) | copy-start | bytes 98308
  51.4 29.5 %copy-start.5 = (bf16[128,128]{1,0:T(8,128)(2,1)S(1)}, bf16[128,128]{1,0:T(8,128)(2,1)}, u32[]{:S(2)}) copy-start(bf16[128,128]{1,0:T(8,128)(2,1)} %param.25) | copy-start | bytes 98308
  51.8 31.0 %copy-start.4 = (bf16[256,256]{1,0:T(8,128)(2,1)S(1)}, bf16[256,256]{1,0:T(8,128)(2,1)}, u32[]{:S(2)}) copy-start(bf16[256,256]{1,0:T(8,128)(2,1)} %get-tuple-element.5) | copy-start | bytes 393220
